TPU v7x, 128 devices: a whole 4x4x4 slice. The times are simulated.
128 devices in a mesh: dp: 32 (over y, z, core), mp: 4 (over x).
Axes of the slice: x: 4, y: 4, z: 4, core: 2. Of those that a mesh axis runs over, the one named last changes fastest.
Arguments:
- grads: bfloat16 [32, 16, 512, 512], P('dp', 'mp'), may hold values from -1000 to 1000, as said below
- block_owner: int32 [4, 4], P('mp'), may hold values from 0 to 63, as said below
- refresh_to: int32 [32, 4, 2], P('dp', 'mp'), may hold values from -1 to 3, as said below
- accum_old: float32 [32, 4, 2, 2, 512, 512], P('dp', 'mp'), may hold values from -0.006 to 60, as said below
- roots_old: float32 [32, 4, 2, 2, 512, 512], P('dp', 'mp'), may hold values from -1 to 1, as said below
Outputs:
- accum_new: float32 [32, 4, 2, 2, 512, 512], P('dp', 'mp')
- roots_new: float32 [32, 4, 2, 2, 512, 512], P('dp', 'mp')
- update: bfloat16 [16, 512, 512], P('mp')
Inputs may be any that keep to these rules, and one draw needn't show every extreme that they name: `grads`: entries are bounded gradient values; rows and columns of a block have different scales. block_owner[c, k] = d * 2 + j puts block k of column c in slot j of dp device d of that column; positions differ within a column; in every column one device holds 2 blocks. `refresh_to`: -1 where the slot holds no block or keeps its previous roots, else a value from 0 to 3; the device holding 2 blocks refreshes all of them. `accum_old`: each matrix is symmetric with a dominant positive diagonal. `roots_old`: each matrix is symmetric with a positive diagonal.
All inputs are finite; a program needn't handle non-finite values.
Results may differ from a plain program's by a relative error of at most 0.0004.
Values may be sent and summed in bfloat16 or wider, within the bound.
A program may use at most 320 MiB of HBM per device.

v0:
```python
import jax
import jax.numpy as jnp
from jax import lax
from jax.sharding import PartitionSpec as P

ITERS = 3


decay_rate = 0.8
epsilon = 1e-06
highest_precision = lax.Precision.HIGHEST


def inverse_root(matrix):
    order_size = matrix.shape[-1]
    identity = jnp.eye(order_size, dtype=matrix.dtype)
    norm_scale = order_size * jnp.sqrt(jnp.mean(matrix * matrix) + epsilon)
    current = matrix / norm_scale
    factor = (5.0 * identity - current) / 4.0
    result = factor * norm_scale ** (-0.25)
    for iteration in range(ITERS - 1):
        square = jnp.dot(factor, factor, precision=highest_precision)
        fourth = jnp.dot(square, square, precision=highest_precision)
        current = jnp.dot(fourth, current, precision=highest_precision)
        factor = (5.0 * identity - current) / 4.0
        result = jnp.dot(result, factor, precision=highest_precision)
    return result


def both_roots(matrices):
    return jnp.stack([inverse_root(matrices[0]), inverse_root(matrices[1])])


def refresh_pair(operands):
    return both_roots(operands[0])


def keep_pair(operands):
    return operands[1]


def per_device(grads, block_owner, refresh_to, accum_old, roots_old):
    n_dp = lax.axis_size("dp")
    n_mp = lax.axis_size("mp")
    my_index = lax.axis_index("dp")
    local = grads[0]
    blocks_here = local.shape[0]
    order_size = local.shape[1]
    slots = accum_old.shape[2]
    owner = block_owner[0]
    places = jnp.arange(n_dp * slots, dtype=jnp.int32).reshape(n_dp, slots)
    chooser = places[:, :, None] == owner[None, None, :]
    mine_places = my_index * slots + jnp.arange(slots, dtype=jnp.int32)
    alive = jnp.any(owner[None, :] == mine_places[:, None], axis=1)
    left_part = jnp.einsum("kac,kbc->kab", local, local, preferred_element_type=jnp.float32)
    right_part = jnp.einsum("kca,kcb->kab", local, local, preferred_element_type=jnp.float32)
    parts = jnp.stack([left_part, right_part, local.astype(jnp.float32)], axis=1)
    shares = lax.psum_scatter(parts, "dp", scatter_dimension=2, tiled=True)
    outgoing = jnp.einsum(
        "djk,kxrc->jxdrc", chooser.astype(jnp.float32), shares, precision=highest_precision
    )
    arrived = lax.all_to_all(outgoing, "dp", split_axis=2, concat_axis=2, tiled=True)
    totals = arrived.reshape(slots, 3, order_size, order_size)
    fresh = totals[:, :2] / float(n_dp * order_size)
    grad_total = totals[:, 2]
    previous = accum_old[0, 0]
    blended = decay_rate * previous + (1.0 - decay_rate) * fresh
    new_accum = jnp.where(alive[:, None, None, None], blended, previous)
    stale = roots_old[0, 0]
    targets = refresh_to[0, 0]
    kept = []
    for position in range(slots):
        kept.append(
            lax.cond(
                targets[position] >= 0,
                refresh_pair,
                keep_pair,
                (new_accum[position], stale[position]),
            )
        )
    roots = jnp.stack(kept)
    partial_product = jnp.einsum(
        "jab,jbc->jac", roots[:, 0], grad_total, precision=highest_precision
    )
    update_full = jnp.einsum(
        "jab,jbc->jac", partial_product, roots[:, 1], precision=highest_precision
    )
    update_square = jnp.sum(update_full * update_full)
    update_norm = lax.psum(update_square, ("dp", "mp"))
    entry_count = float(blocks_here * n_mp * order_size * order_size)
    ratio = 1.0 / jnp.sqrt(update_norm / entry_count + epsilon)
    scaled = (ratio * update_full).astype(jnp.bfloat16)
    rows_each = order_size // n_dp
    sending = scaled.reshape(slots, n_dp, rows_each, order_size)
    gotten = lax.all_to_all(sending, "dp", split_axis=1, concat_axis=1, tiled=True)
    picked = jnp.einsum(
        "djk,jdrc->krc", chooser.astype(jnp.bfloat16), gotten, preferred_element_type=jnp.float32
    ).astype(jnp.bfloat16)
    update = lax.all_gather(picked, "dp", axis=1, tiled=True)
    return (new_accum[None, None], roots[None, None], update)


def solution(mesh):
    in_specs = (
        P("dp", "mp", None, None),
        P("mp", None),
        P("dp", "mp", None),
        P("dp", "mp", None, None, None, None),
        P("dp", "mp", None, None, None, None),
    )
    out_specs = (
        P("dp", "mp", None, None, None, None),
        P("dp", "mp", None, None, None, None),
        P("mp", None, None),
    )
    return jax.shard_map(
        per_device, mesh=mesh, in_specs=in_specs, out_specs=out_specs, check_vma=False
    )
```

profile of v0, /device:TPU:1, one launch (start us, length us, event | category | flops | bytes accessed | tf_op | source)
XLA Modules:
  0.0 496.9 jit_solution(11251758081117201339)
XLA Ops:
  7.2 0.0 reduce-scatter.2.cloned.1.call-start
  7.2 4.3 bitcast_convert_fusion
  11.6 3.3 convolution_bitcast_fusion.5
  14.9 3.2 convolution_bitcast_fusion.6
  18.1 10.7 %pad_maximum_fusion = f32[4,3,512,512]{3,2,0,1:T(8,128)} fusion(f32[4,1,512,512]{3,2,0,1:T(8,128)} %bitcast_convert_fusion, f32[4,1,512,512]{3,2,0,1:T(8,128)} %convolution_bitcast_fusion.5, f32[4,1,512,512]{3,2,0,1:T(8,128)} %convolution_bitcast_fusion.6), kind=kLoop, calls=%fused_computation.160 | loop fusion | flops 6291456 | bytes 25165824 | tf_op jit(solution)/shard_map/stack | solution.py:57
  28.9 0.0 reduce-scatter.2.cloned.1.call-update
  28.9 106.7 %reduce-scatter.2.cloned.1.call-done = f32[4,3,16,512]{3,2,0,1:T(8,128)} async-done(((f32[4,3,512,512]{3,2,0,1:T(8,128)}), f32[4,3,16,512]{3,2,0,1:T(8,128)}) %reduce-scatter.2.cloned.1.call-update) | async-done | bytes 393232 | tf_op jit(solution)/shard_map/reduce_scatter | solution.py:58
  135.6 4.5 convolution_bitcast_fusion.4
  140.2 7.5 %copy.36 = f32[2,3,32,16,512]{4,0,3,1,2:T(2,128)} copy(f32[2,3,32,16,512]{4,2,0,3,1:T(8,128)S(1)} %convolution_bitcast_fusion.4) | data formatting | bytes 12582912 | tf_op jit(solution)/shard_map/djk,kxrc->jxdrc/transpose | solution.py:59
  147.7 7.4 %all-to-all-start = ((f32[2,3,32,16,512]{4,0,3,1,2:T(2,128)}), f32[2,3,32,16,512]{4,0,3,1,2:T(2,128)}, u32[]{:S(2)}, u32[]{:S(2)}) async-start(f32[2,3,32,16,512]{4,0,3,1,2:T(2,128)} %copy.36), calls=%async_computation.1 | async-start | bytes 12582912 | tf_op jit(solution)/shard_map/all_to_all | solution.py:62
  155.1 0.0 all-gather.2.cloned.1.call-start
  155.1 0.6 fusion.162
  157.0 0.2 compare_reduce_fusion
  157.2 75.8 %all-to-all-done = f32[2,3,32,16,512]{4,0,3,1,2:T(2,128)} async-done(((f32[2,3,32,16,512]{4,0,3,1,2:T(2,128)}), f32[2,3,32,16,512]{4,0,3,1,2:T(2,128)}, u32[]{:S(2)}, u32[]{:S(2)}) %all-to-all-start) | async-done | bytes 6291488 | tf_op jit(solution)/shard_map/all_to_all | solution.py:62
  233.0 4.1 copy.37
  237.2 3.2 fusion.142
  240.4 9.0 %conditional.2 = (f32[1,2,512,512]{3,2,1,0:T(8,128)S(1)}) conditional(s32[]{:T(128)} %bitcast.32, f32[1,1,2,2,512,512]{5,4,3,2,1,0:T(8,128)S(1)} %copy-done.5, f32[2,2,512,512]{3,2,1,0:T(8,128)} %fusion.142), branch_computations={%region_2.3_spmd, %region_3.6_spmd} | conditional | flops 25783435264 | bytes 48234680 | solution.py:74
  240.4 0.2 slice_bitcast_fusion
  249.4 11.8 %conditional.3 = (f32[1,2,512,512]{3,2,1,0:T(8,128)}) conditional(s32[]{:T(128)} %bitcast.34, f32[1,1,2,2,512,512]{5,4,3,2,1,0:T(8,128)} %param.13, f32[2,2,512,512]{3,2,1,0:T(8,128)} %fusion.142), branch_computations={%region_6.7_spmd, %region_7.10_spmd} | conditional | flops 25783435264 | bytes 60817676 | solution.py:74
  249.4 3.1 slice_bitcast_fusion.1
  261.2 4.1 copy.51
  265.3 3.5 fusion.145
  268.9 5.5 %multiply_reduce_fusion.4 = (f32[]{:T(128)}, f32[2,512,512]{2,1,0:T(8,128)}) fusion(f32[2,512,512]{2,1,0:T(8,128)S(1)} %fusion.145, f32[1,2,512,512]{3,2,0,1:T(8,128)S(1)} %bitcast.169, f32[1,2,512,512]{3,2,0,1:T(8,128)S(1)} %bitcast.173), kind=kOutput, calls=%fused_computation.185 | convolution fusion | flops 3222798336 | bytes 8388612 | tf_op jit(solution)/shard_map/jab,jbc->jac/dot_general | solution.py:85
  274.4 145.0 %psum.7 = f32[]{:T(128)} all-reduce(f32[]{:T(128)} %get-tuple-element.43), channel_id=1, replica_groups=mesh['dp'=32,'mp'=4] {'dp','mp'}, use_global_device_ids=true, to_apply=%region_11.12 | all-reduce | flops 1 | bytes 8 | tf_op jit(solution)/shard_map/psum | solution.py:89
  420.0 1.9 multiply_convert_fusion
  421.8 1.1 copy.41
  422.9 21.7 %all_to_all.10 = bf16[2,32,16,512]{3,0,2,1:T(2,128)(2,1)S(1)} all-to-all(bf16[2,32,16,512]{3,0,2,1:T(2,128)(2,1)S(1)} %copy.41), channel_id=1, replica_groups=mesh['dp'=32,'mp'=4] {'dp'}, dimensions={1} | all-to-all | bytes 2097152 | tf_op jit(solution)/shard_map/all_to_all | solution.py:95
  444.6 1.3 fusion.153
  446.0 2.2 fusion.140
  448.2 2.5 copy.43
  450.7 35.9 %all-gather.2.cloned.1.call-done = bf16[4,512,512]{2,0,1:T(4,128)(2,1)} async-done(((bf16[4,16,512]{2,0,1:T(4,128)(2,1)}), bf16[4,512,512]{2,0,1:T(4,128)(2,1)}) %all-gather.2.cloned.1.call-update) | async-done | bytes 2097168 | tf_op jit(solution)/shard_map/all_gather | solution.py:99
  486.6 3.3 copy.44
  (15 shorter events, 0.1 us)
Async XLA Ops:
  7.2 4.4 copy-start.1
  7.2 128.4 %reduce-scatter.2.cloned.1.call-start = ((), (), s32[]{:S(2)}) async-start(), calls=%async_computation.3 | async-start | bytes 12976128 | tf_op jit(solution)/shard_map/reduce_scatter | solution.py:58
  28.9 106.7 %copy-start.7 = (s32[1,4]{1,0:T(1,128)S(1)}, s32[1,4]{1,0:T(1,128)}, u32[]{:S(2)}) copy-start(s32[1,4]{1,0:T(1,128)} %param.10) | copy-start | bytes 52
  147.7 7.5 %copy-start.8 = (s32[1,1,2]{2,1,0:T(1,128)S(1)}, s32[1,1,2]{2,1,0:T(1,128)}, u32[]{:S(2)}) copy-start(s32[1,1,2]{2,1,0:T(1,128)} %param.11) | copy-start | bytes 28
  147.7 85.4 %all-to-all-start = ((f32[2,3,32,16,512]{4,0,3,1,2:T(2,128)}), f32[2,3,32,16,512]{4,0,3,1,2:T(2,128)}, u32[]{:S(2)}, u32[]{:S(2)}) async-start(f32[2,3,32,16,512]{4,0,3,1,2:T(2,128)} %copy.36), calls=%async_computation.1 | async-start | bytes 12582912 | tf_op jit(solution)/shard_map/all_to_all | solution.py:62
  155.1 331.5 %all-gather.2.cloned.1.call-start = ((), (), s32[]{:S(2)}) async-start(), calls=%async_computation.4 | async-start | bytes 2162688 | tf_op jit(solution)/shard_map/all_gather | solution.py:99
  233.0 4.2 copy-start.4
  237.2 3.2 copy-start.5
  261.2 4.2 copy-start
Sparse Core Ops, SparseCore 0:
  29.0 106.5 reduce-scatter.1
  446.1 40.4 all-gather.1
where the time goes:
time: 505 us; the launch traced here: 497 us
  waiting for transfers between devices  218 us (43%)
  blocking collectives  167 us (33%)
  local copies, waits for them, and re-layouts  26.5 us (5%)
  other arithmetic  22.6 us (4%)
  matrix products  21.5 us (4%)
  loops' own time  17.5 us (3%)
  between operations  16.3 us (3%)
  starting transfers between devices  7.48 us (1%)
    psum x1, blocking collectives, per_device(): update_norm = lax.psum(update_square, ('dp', 'mp'))  145 us
    reduce_scatter x1, waiting for transfers between devices, per_device(): shares = lax.psum_scatter(parts, 'dp', scatter_dimension=2, tiled=True)  107 us
    all_to_all x1, waiting for transfers between devices, per_device(): lax.all_to_all(outgoing, 'dp', split_axis=2, concat_axis=2, tiled=True)  75.8 us
    all_gather x1, waiting for transfers between devices, per_device(): update = lax.all_gather(picked, 'dp', axis=1, tiled=True)  35.9 us
    all_to_all x1, blocking collectives, per_device(): lax.all_to_all(sending, 'dp', split_axis=1, concat_axis=1, tiled=True)  21.7 us
    another operation x2, loops' own time, per_device(): lax.cond(targets[position] >= 0, refresh_pair, keep_pair, (new_accum[posi...  17.5 us
    another operation x1, other arithmetic, per_device(): jnp.stack([left_part, right_part, local.astype(jnp.float32)], axis=1)  10.7 us
  transfers between devices with their start and end apart: 3, of which 3 were waited for; matrix products, arithmetic and copies ran while one was open for 1% of the time, Pallas kernels for 0%

commit v1 on v0

v1 whole, which is shorter than its diff:
```python
import functools

import jax
import jax.numpy as jnp
from jax import lax
from jax.experimental import pallas as pl
from jax.experimental.pallas import tpu as pltpu
from jax.sharding import PartitionSpec as P

MESH = pl.DeviceIdType.MESH
F32 = jnp.float32
BF16 = jnp.bfloat16

BS = 512
KB = 4
SLOTS = 2
TL = 128
TILES = [(a, b) for a in range(4) for b in range(a, 4)]
NT = len(TILES)
SP = 5
GP = 4
decay_rate = 0.8
epsilon = 1e-06


def coords():
    d = lax.axis_index("dp")
    return d // 8, (d // 2) % 4, d % 2


def at(y, z, c):
    return {"dp": (y * 4 + z) * 2 + c}


def dot_nt(a, b):
    return lax.dot_general(a, b, (((1,), (1,)), ((), ())), preferred_element_type=F32)


def dot_tn(a, b):
    return lax.dot_general(a, b, (((0,), (0,)), ((), ())), preferred_element_type=F32)


def dot_nn(a, b):
    return lax.dot_general(a, b, (((1,), (0,)), ((), ())), preferred_element_type=F32)


def stats_kernel(
    g_ref, rf_ref, acc_ref, o_ref, gq_ref, pacc_ref, prf_ref,
    praw, st, r1, r2, f3,
    s_raw, s_rf, s_acc, s1, q1, s2, q2, s3, q3, s4, q4, sd, qd, sl,
):
    y, z, c = coords()
    pos1 = z + c * (y - z)
    pos2 = y + c * (z - y)

    def dev1(p):
        return at(y + c * (p - y), p + c * (z - p), c)

    def dev2(p):
        return at(p + c * (y - p), z + c * (p - z), c)

    mate = at(y, z, 1 - c)

    barrier = pltpu.get_barrier_semaphore()
    for o in (1, 2, 3):
        pl.semaphore_signal(barrier, inc=1, device_id=dev1((pos1 + o) % 4), device_id_type=MESH)
        pl.semaphore_signal(barrier, inc=1, device_id=dev2((pos2 + o) % 4), device_id_type=MESH)
    pl.semaphore_signal(barrier, inc=1, device_id=mate, device_id_type=MESH)
    pl.semaphore_wait(barrier, 7)

    def rcopy(src, dst, ss, rs, device):
        return pltpu.make_async_remote_copy(
            src_ref=src, dst_ref=dst, send_sem=ss, recv_sem=rs, device_id=device, device_id_type=MESH
        )

    raw = rcopy(g_ref.at[pl.ds(2 * (1 - c), 2)], praw, s_raw.at[0], s_raw.at[1], mate)
    raw.start()
    accs = [
        rcopy(acc_ref.at[j, 1], pacc_ref.at[j], s_acc.at[0, j], s_acc.at[1, j], mate) for j in range(SLOTS)
    ]
    flags = rcopy(rf_ref, prf_ref, s_rf.at[0], s_rf.at[1], mate)
    flags.start()
    for a in accs:
        a.start()

    def c1(p, o, q):
        return rcopy(st.at[p, q], r1.at[o - 1, q], s1.at[o - 1, q], q1.at[o - 1, q], dev1(p))

    raw.wait()

    def put(p, a, b, block):
        t = TILES.index((a, b))
        for half in range(2):
            h = 2 * t + half
            st[p, h // SP, h % SP] = block[half * 64:(half + 1) * 64]

    def quadrants(p, quad):
        x = quad(0, 0)
        put(p, 0, 0, x[:128, :128])
        put(p, 0, 1, x[:128, 128:])
        put(p, 1, 1, x[128:, 128:])
        x = quad(0, 1)
        put(p, 0, 2, x[:128, :128])
        put(p, 0, 3, x[:128, 128:])
        put(p, 1, 2, x[128:, :128])
        put(p, 1, 3, x[128:, 128:])
        x = quad(1, 1)
        put(p, 2, 2, x[:128, :128])
        put(p, 2, 3, x[:128, 128:])
        put(p, 3, 3, x[128:, 128:])

    @pl.loop(0, 4)
    def _(i):
        p = (pos1 + jnp.where(i == 0, 2, jnp.where(i == 1, 1, jnp.where(i == 2, 3, 0)))) % 4
        o = (pos1 - p + 4) % 4
        blk = p // 2
        lr = p % 2

        @pl.when(lr == 0)
        def _():
            quadrants(
                p,
                lambda a, b: dot_nt(
                    g_ref[2 * c + blk, a * 256:(a + 1) * 256, :], g_ref[2 * c + blk, b * 256:(b + 1) * 256, :]
                )
                + dot_nt(praw[blk, a * 256:(a + 1) * 256, :], praw[blk, b * 256:(b + 1) * 256, :]),
            )

        @pl.when(lr == 1)
        def _():
            quadrants(
                p,
                lambda a, b: dot_tn(
                    g_ref[2 * c + blk, :, a * 256:(a + 1) * 256], g_ref[2 * c + blk, :, b * 256:(b + 1) * 256]
                )
                + dot_tn(praw[blk, :, a * 256:(a + 1) * 256], praw[blk, :, b * 256:(b + 1) * 256]),
            )

        for q in range(4):
            rows = pl.ds(lr * 256 + q * 64, 64)
            total = g_ref[2 * c + blk, rows, :].astype(F32) + praw[blk, rows, :].astype(F32)
            for k in range(GP):
                st[p, q, SP + k] = total[:, k * 128:(k + 1) * 128]

        @pl.when(i < 3)
        def _():
            for k in range(4):
                q = (pos2 + 1 + k) % 4
                c1(p, o, q).start()

    def c2(q):
        o = (pos2 - q + 4) % 4
        return rcopy(st.at[pos1, q], r2.at[o - 1], s2.at[o - 1], q2.at[o - 1], dev2(q))

    @pl.loop(1, 5)
    def _(k):
        q = (pos2 + k) % 4
        for o in (1, 2, 3):
            c1(pos1, o, q).wait_recv()
        st[pos1, q] = (st[pos1, q] + r1[0, q]) + (r1[1, q] + r1[2, q])

        @pl.when(k < 4)
        def _():
            c2(q).start()

    for o in (1, 2, 3):
        c2((pos2 + o) % 4).wait_recv()
    f3[pos2] = (st[pos1, pos2] + r2[0]) + (r2[1] + r2[2])

    def c3(o):
        return rcopy(f3.at[pos2], f3.at[pos2], s3.at[o - 1], q3.at[o - 1], dev2((pos2 - o + 4) % 4))

    def c4(o, q):
        return rcopy(
            f3.at[q, pl.ds(0, SP)], o_ref.at[c, pos1, q], s4.at[o - 1, q], q4.at[o - 1, q],
            dev1((pos1 - o + 4) % 4),
        )

    def cd_own(q):
        return rcopy(f3.at[q, pl.ds(0, SP)], o_ref.at[c, pos1, q], sd.at[0, q], qd.at[0, q], mate)

    def cd(o, q):
        p = (pos1 + o) % 4
        return rcopy(o_ref.at[c, p, q], o_ref.at[c, p, q], sd.at[o, q], qd.at[o, q], mate)

    def keep(q):
        return pltpu.make_async_copy(f3.at[q, pl.ds(0, SP)], o_ref.at[c, pos1, q], sl.at[0, q])

    def keep_g(q):
        return pltpu.make_async_copy(f3.at[q, pl.ds(SP, GP)], gq_ref.at[q], sl.at[1, q])

    for o in (2, 1, 3):
        c3(o).start()

    for k, o in ((0, 0), (1, 1), (3, 3), (2, 2)):
        q = (pos2 + k) % 4
        if k:
            rcopy(f3.at[pos2], f3.at[q], s3.at[o - 1], q3.at[o - 1], dev2(q)).wait_recv()
        for oo in (2, 1, 3):
            c4(oo, q).start()
        cd_own(q).start()
        keep(q).start()
        keep_g(q).start()

    for o in (1, 3, 2):
        for k in (0, 1, 3, 2):
            q = (pos2 + k) % 4
            p = (pos1 + o) % 4
            rcopy(
                f3.at[q, pl.ds(0, SP)], o_ref.at[c, p, q], s4.at[o - 1, q], q4.at[o - 1, q], dev1(p)
            ).wait_recv()
            cd(o, q).start()

    flags.wait()
    for a in accs:
        a.wait()
    for k in range(1, 4):
        p = (pos1 + k) % 4
        for q in range(4):
            c1(p, (pos1 - p + 4) % 4, q).wait_send()
        c2((pos2 + k) % 4).wait_send()
        c3(k).wait_send()
    for q in range(4):
        keep(q).wait()
        keep_g(q).wait()
        for o in (1, 2, 3):
            c4(o, q).wait_send()
        own = cd_own(q)
        own.wait_send()
        rcopy(f3.at[q, pl.ds(0, SP)], o_ref.at[1 - c, pos2, q], sd.at[0, q], qd.at[0, q], mate).wait_recv()
        for o in (1, 2, 3):
            cd(o, q).wait_send()
    for q in range(4):
        for o in (1, 2, 3):
            p = (pos2 + o) % 4
            rcopy(o_ref.at[1 - c, p, q], o_ref.at[1 - c, p, q], sd.at[o, q], qd.at[o, q], mate).wait_recv()


def call_stats(grads, refresh, acc):
    dma = pltpu.SemaphoreType.DMA
    return pl.pallas_call(
        stats_kernel,
        name="stats",
        out_shape=(
            jax.ShapeDtypeStruct((2, 4, 4, SP, 64, TL), F32),
            jax.ShapeDtypeStruct((4, GP, 64, TL), F32),
            jax.ShapeDtypeStruct((SLOTS, BS, BS), F32),
            jax.ShapeDtypeStruct((8, TL), jnp.int32),
        ),
        in_specs=[pl.BlockSpec(memory_space=pltpu.VMEM)] * 2 + [pl.BlockSpec(memory_space=pl.ANY)],
        out_specs=(pl.BlockSpec(memory_space=pl.ANY),) * 3 + (pl.BlockSpec(memory_space=pltpu.VMEM),),
        scratch_shapes=[
            pltpu.VMEM((2, BS, BS), BF16),
            pltpu.VMEM((4, 4, SP + GP, 64, TL), F32),
            pltpu.VMEM((3, 4, SP + GP, 64, TL), F32),
            pltpu.VMEM((3, SP + GP, 64, TL), F32),
            pltpu.VMEM((4, SP + GP, 64, TL), F32),
            dma((2,)), dma((2,)), dma((2, SLOTS)),
            dma((3, 4)), dma((3, 4)), dma((3,)), dma((3,)), dma((3,)), dma((3,)),
            dma((3, 4)), dma((3, 4)), dma((4, 4)), dma((4, 4)), dma((2, 4)),
        ],
        compiler_params=pltpu.CompilerParams(
            collective_id=1, has_side_effects=True, vmem_limit_bytes=40 << 20
        ),
    )(grads, refresh, acc)


def split(x):
    hi = x.astype(BF16)
    return hi, (x - hi.astype(F32)).astype(BF16)


def dot3(ah, al, bh, bl):
    return dot_nn(ah, bh) + (dot_nn(ah, bl) + dot_nn(al, bh))


def find_slot(owner_ref, place):
    block = jnp.int32(0)
    alive = jnp.int32(0)
    for k in range(KB):
        hit = (owner_ref[0, k] == place).astype(jnp.int32)
        block = block + k * hit
        alive = alive + hit
    return block, alive


def roots_kernel(
    owner_ref, rf_ref, prf_ref, st_ref, acc_ref, pacc_ref, old_ref,
    new_ref, lroot_ref, rroot_ref,
    flag, a_buf, s_buf, mf, tf, m1f, vf, mh, ml, th, tl, uh, ul, m1h, m1l, vh, vl, xbuf,
    sem_a, sem_s, sem_o, sem_r,
):
    d = lax.axis_index("dp")
    mate = d + 1 - 2 * (d % 2)
    for j in range(SLOTS):
        blk, alive = find_slot(owner_ref, d * SLOTS + j)
        fresh = alive * (rf_ref[0, j] >= 0).astype(jnp.int32)
        pblk, palive = find_slot(owner_ref, mate * SLOTS + j)
        pfresh = palive * (prf_ref[0, j] >= 0).astype(jnp.int32)
        flag[0, j], flag[0, 4 + j], flag[0, 2 + j] = blk, blk, pblk
        flag[1, j], flag[1, 4 + j], flag[1, 2 + j] = alive, alive, pfresh
        flag[2, j], flag[2, 2 + j] = fresh, pfresh

    flag[3, 0] = jnp.int32(0)

    def old(i):
        if 2 <= i < 4:
            return pacc_ref.at[i - 2]
        return acc_ref.at[i % 2, i // 4]

    for i in (0, 1, 2, 3, 4, 5):
        pltpu.make_async_copy(old(i), a_buf.at[i], sem_a.at[i]).start()
        lr = 0 if i < 2 else 1
        pltpu.make_async_copy(st_ref.at[flag[0, i], lr], s_buf.at[i], sem_s.at[i]).start()
    for j in range(SLOTS):
        @pl.when(flag[2, j] == 0)
        def _():
            pltpu.make_async_copy(old_ref.at[j, 0], lroot_ref.at[j], sem_r.at[j]).start()

    @pl.loop(0, 6)
    def _(i):
        pltpu.make_async_copy(acc_ref.at[0, 0], a_buf.at[i], sem_a.at[i]).wait()
        pltpu.make_async_copy(st_ref.at[0, 0], s_buf.at[i], sem_s.at[i]).wait()

        @pl.when(flag[1, i] == 1)
        def _():
            for t, (a, b) in enumerate(TILES):
                fresh = s_buf[i, t] * F32((1.0 - decay_rate) / 16384.0)
                ra, rb = pl.ds(a * TL, TL), pl.ds(b * TL, TL)
                a_buf[i, ra, rb] = decay_rate * a_buf[i, ra, rb] + fresh
                if a != b:
                    a_buf[i, rb, ra] = decay_rate * a_buf[i, rb, ra] + fresh.T

    outs = [pltpu.make_async_copy(a_buf.at[i], new_ref.at[i % 2, i // 4], sem_o.at[i]) for i in (0, 1, 4, 5)]
    for o in outs:
        o.start()

    half = BS // 2
    c4 = 625.0 / 256.0

    def each(fn):
        @pl.loop(0, 2)
        def _(h):
            fn(pl.ds(pl.multiple_of(h * half, half), half))

    def put(ref, hi, lo, rows, x):
        if ref is not None:
            ref[rows, :] = x
        hi[rows, :], lo[rows, :] = split(x)

    def mul(rows, ah, al, bh, bl):
        return dot3(ah[rows, :], al[rows, :], bh[...], bl[...])

    @pl.loop(0, 4)
    def _(t):
        @pl.when(flag[2, t] == 1)
        def _():
            a = a_buf[t]
            square = jnp.sum(a * a, axis=0, keepdims=True)
            mean = jnp.sum(square, axis=1, keepdims=True) * (1.0 / (BS * BS))
            scale = BS * jnp.sqrt(mean + epsilon)
            inverse = 1.0 / scale
            outer = 1.0 / jnp.sqrt(jnp.sqrt(scale))

            def start(rows):
                put(mf, mh, ml, rows, a_buf[t, rows, :] * inverse)

            each(start)

            def first(rows):
                q = mul(rows, mh, ml, mh, ml)
                put(tf, th, tl, rows, (q - 10.0 * mf[rows, :]) * (1.0 / 16.0))

            each(first)

            def second(rows):
                q = mul(rows, th, tl, th, tl)
                put(None, uh, ul, rows, (25.0 / 8.0) * tf[rows, :] + q)

            each(second)

            def third(rows):
                q = mul(rows, uh, ul, mh, ml)
                put(m1f, m1h, m1l, rows, c4 * mf[rows, :] + q)

            each(third)

            def fourth(rows):
                q = mul(rows, m1h, m1l, m1h, m1l)
                put(tf, th, tl, rows, (q - 10.0 * m1f[rows, :]) * (1.0 / 16.0))
                q = mul(rows, mh, ml, m1h, m1l)
                put(vf, vh, vl, rows, q * (1.0 / 16.0) - (5.0 / 16.0) * (mf[rows, :] + m1f[rows, :]))

            each(fourth)

            each(second)

            def seventh(rows):
                q = mul(rows, uh, ul, m1h, m1l)
                put(mf, mh, ml, rows, c4 * m1f[rows, :] + q)

            each(seventh)

            @pl.when(flag[3, 0] == 1)
            def _():
                pltpu.make_async_copy(xbuf, rroot_ref.at[0], sem_r.at[2]).wait()

            flag[3, 0] = jnp.int32(1)

            def last(rows):
                q = mul(rows, vh, vl, mh, ml)
                x = 1.25 * vf[rows, :] - (25.0 / 64.0) * mf[rows, :] - 0.25 * q
                r = lax.broadcasted_iota(jnp.int32, (half, BS), 0) + rows.start
                k = lax.broadcasted_iota(jnp.int32, (half, BS), 1)
                xbuf[rows, :] = outer * (x + jnp.where(r == k, F32(125.0 / 64.0), F32(0.0)))

            each(last)

            @pl.when(t < 2)
            def _():
                pltpu.make_async_copy(xbuf, lroot_ref.at[t % 2], sem_r.at[2]).start()

            @pl.when(t >= 2)
            def _():
                pltpu.make_async_copy(xbuf, rroot_ref.at[t % 2], sem_r.at[2]).start()

    @pl.when(flag[3, 0] == 1)
    def _():
        pltpu.make_async_copy(xbuf, rroot_ref.at[0], sem_r.at[2]).wait()
    for j in range(SLOTS):
        @pl.when(flag[2, j] == 0)
        def _():
            pltpu.make_async_copy(old_ref.at[j, 0], lroot_ref.at[j], sem_r.at[j]).wait()
    for o in outs:
        o.wait()


def call_roots(owner, refresh, prefresh, stats, acc, pacc, old):
    dma = pltpu.SemaphoreType.DMA
    anywhere = pl.BlockSpec(memory_space=pl.ANY)
    smem = pl.BlockSpec(memory_space=pltpu.SMEM)
    full = lambda dt: pltpu.VMEM((BS, BS), dt)
    return pl.pallas_call(
        roots_kernel,
        name="roots",
        out_shape=(
            jax.ShapeDtypeStruct((SLOTS, 2, BS, BS), F32),
            jax.ShapeDtypeStruct((SLOTS, BS, BS), F32),
            jax.ShapeDtypeStruct((SLOTS, BS, BS), F32),
        ),
        in_specs=[smem] * 3 + [anywhere] * 4,
        out_specs=(anywhere,) * 3,
        scratch_shapes=[
            pltpu.SMEM((4, 8), jnp.int32),
            pltpu.VMEM((6, BS, BS), F32),
            pltpu.VMEM((6, NT, TL, TL), F32),
        ]
        + [full(F32)] * 4 + [full(BF16)] * 10 + [full(F32)]
        + [dma((6,)), dma((6,)), dma((6,)), dma((3,))],
        compiler_params=pltpu.CompilerParams(vmem_limit_bytes=40 << 20),
        cost_estimate=pl.CostEstimate(flops=20 * 10**9, bytes_accessed=20 << 20, transcendentals=0),
    )(owner, refresh, prefresh, stats, acc, pacc, old)


def product_kernel(
    owner_ref, rf_ref, l_ref, r_ref, old_ref, *rest,
):
    g_refs = rest[:8]
    roots_ref, sq_ref, p_ref, flag, lbuf, rbuf, gbuf, gh, gl, sem = rest[8:]
    d = lax.axis_index("dp")
    c = d % 2
    pos1 = (d // 2) % 4 + c * (d // 8 - (d // 2) % 4)
    pos2 = d // 8 + c * ((d // 2) % 4 - d // 8)
    outs = []
    for j in range(SLOTS):
        blk, alive = find_slot(owner_ref, d * SLOTS + j)
        fresh = alive * (rf_ref[0, j] >= 0).astype(jnp.int32)
        flag[0, j], flag[1, j] = alive, fresh
        pltpu.make_async_copy(l_ref.at[j], lbuf.at[j], sem.at[j, 0]).start()

        @pl.when(fresh == 1)
        def _():
            pltpu.make_async_copy(r_ref.at[j], rbuf.at[j], sem.at[j, 1]).start()

        @pl.when(fresh == 0)
        def _():
            pltpu.make_async_copy(old_ref.at[j, 1], rbuf.at[j], sem.at[j, 1]).start()

        mine = (blk // 2 == c).astype(jnp.int32)
        for h in range(2):
            p = 2 * (blk % 2) + h
            o = lax.rem(p - jnp.where(mine == 1, pos1, pos2) + 4, 4)
            for i in range(8):
                @pl.when((o == i % 4) & (mine == 1 - i // 4))
                def _():
                    pltpu.make_async_copy(g_refs[i], gbuf.at[j, h], sem.at[j, 2 + h]).start()
    for j in range(SLOTS):
        pltpu.make_async_copy(l_ref.at[j], lbuf.at[j], sem.at[j, 0]).wait()
        outs.append(pltpu.make_async_copy(lbuf.at[j], roots_ref.at[j, 0], sem.at[j, 4]))
        outs[-1].start()
    sq_ref[...] = jnp.zeros_like(sq_ref)
    for j in range(SLOTS):
        pltpu.make_async_copy(r_ref.at[j], rbuf.at[j], sem.at[j, 1]).wait()
        for h in range(2):
            pltpu.make_async_copy(g_refs[0], gbuf.at[j, h], sem.at[j, 2 + h]).wait()
        outs.append(pltpu.make_async_copy(rbuf.at[j], roots_ref.at[j, 1], sem.at[j, 5]))
        outs[-1].start()

    @pl.loop(0, SLOTS)
    def _(j):
        @pl.when(flag[0, j] == 1)
        def _():
            for h in range(2):
                for q in range(4):
                    for k in range(4):
                        rows, cols = pl.ds(h * 256 + q * 64, 64), pl.ds(k * TL, TL)
                        gh[0, rows, cols], gl[0, rows, cols] = split(gbuf[j, h, q, k])
            gh[1], gl[1] = split(rbuf[j])

            @pl.loop(0, 2)
            def _(h):
                rows = pl.ds(pl.multiple_of(h * 256, 256), 256)
                ah, al = split(lbuf[j, rows, :])
                t = dot3(ah, al, gh[0], gl[0])
                th, tl = split(t)
                x = dot3(th, tl, gh[1], gl[1])
                p_ref[j, rows, :] = x
                part = jnp.sum((x * x).reshape(32, 8, BS), axis=0)
                sq_ref[...] += (part[:, :128] + part[:, 128:256]) + (part[:, 256:384] + part[:, 384:])

        @pl.when(flag[0, j] == 0)
        def _():
            p_ref[j] = jnp.zeros((BS, BS), F32)

    for o in outs:
        o.wait()


def call_product(owner, refresh, lroot, rroot, old, pieces):
    anywhere = pl.BlockSpec(memory_space=pl.ANY)
    smem = pl.BlockSpec(memory_space=pltpu.SMEM)
    vmem = pl.BlockSpec(memory_space=pltpu.VMEM)
    return pl.pallas_call(
        product_kernel,
        name="product",
        out_shape=(
            jax.ShapeDtypeStruct((SLOTS, 2, BS, BS), F32),
            jax.ShapeDtypeStruct((8, TL), F32),
            jax.ShapeDtypeStruct((SLOTS, BS, BS), F32),
        ),
        in_specs=[smem] * 2 + [anywhere] * 11,
        out_specs=(anywhere, vmem, vmem),
        scratch_shapes=[
            pltpu.SMEM((2, 2), jnp.int32),
            pltpu.VMEM((SLOTS, BS, BS), F32),
            pltpu.VMEM((SLOTS, BS, BS), F32),
            pltpu.VMEM((SLOTS, 2, 4, GP, 64, TL), F32),
            pltpu.VMEM((2, BS, BS), BF16),
            pltpu.VMEM((2, BS, BS), BF16),
            pltpu.SemaphoreType.DMA((SLOTS, 6)),
        ],
        compiler_params=pltpu.CompilerParams(vmem_limit_bytes=40 << 20),
    )(owner, refresh, lroot, rroot, old, *pieces)


def permute(x, n, place):
    pairs = []
    for d in range(n):
        y, z, c = d // 8, (d // 2) % 4, d % 2
        pairs.append((d, place(y, z, c)))
    return lax.ppermute(x, "dp", pairs)


def number(y, z, c):
    return ((y % 4) * 4 + z % 4) * 2 + c


def per_device(grads, block_owner, refresh_to, accum_old, roots_old):
    n_dp = lax.axis_size("dp")
    n_mp = lax.axis_size("mp")
    my_index = lax.axis_index("dp")
    acc, old = accum_old[0, 0], roots_old[0, 0]
    refresh = jnp.pad(refresh_to[0], ((0, 7), (0, TL - SLOTS)))
    stats, gq, pacc, prefresh = call_stats(grads[0], refresh, acc)
    stats = stats.reshape(KB, 2, NT, TL, TL)
    new_accum, lroot, rroot = call_roots(block_owner, refresh, prefresh, stats, acc, pacc, old)
    line = [gq]
    for o in (1, 2, 3):
        line.append(permute(gq, n_dp, lambda y, z, c: number(y - o * c, z - o * (1 - c), c)))
    swap = lambda y, z, c: number(y, z, 1 - c)
    pieces = line + [permute(x, n_dp, swap) for x in line]
    rroot = permute(rroot, n_dp, swap)
    roots, sq, product = call_product(block_owner, refresh, lroot, rroot, old, pieces)

    update_norm = lax.psum(jnp.sum(sq), ("dp", "mp"))
    ratio = 1.0 / jnp.sqrt(update_norm / float(KB * n_mp * BS * BS) + epsilon)
    scaled = (ratio * product).astype(BF16)
    places = jnp.arange(n_dp * SLOTS, dtype=jnp.int32).reshape(n_dp, SLOTS)
    chooser = places[:, :, None] == block_owner[0][None, None, :]
    sending = scaled.reshape(SLOTS, n_dp, BS // n_dp, BS)
    gotten = lax.all_to_all(sending, "dp", split_axis=1, concat_axis=1, tiled=True)
    picked = jnp.einsum(
        "djk,jdrc->krc", chooser.astype(BF16), gotten, preferred_element_type=F32
    ).astype(BF16)
    update = lax.all_gather(picked, "dp", axis=1, tiled=True)
    return (new_accum[None, None], roots[None, None], update)


def solution(mesh):
    in_specs = (
        P("dp", "mp", None, None),
        P("mp", None),
        P("dp", "mp", None),
        P("dp", "mp", None, None, None, None),
        P("dp", "mp", None, None, None, None),
    )
    out_specs = (
        P("dp", "mp", None, None, None, None),
        P("dp", "mp", None, None, None, None),
        P("mp", None, None),
    )
    return jax.shard_map(
        per_device, mesh=mesh, in_specs=in_specs, out_specs=out_specs, check_vma=False
    )
```

time: 505 us -> 279 us (0.55); the launches traced: 497 us -> 278 us
  waiting for transfers between devices: 218 us -> 71.6 us
  blocking collectives: 167 us -> 83.4 us
  Pallas kernels: 0 us -> 82.9 us
  other arithmetic: 22.6 us -> 0.89 us
  matrix products: 21.5 us -> 1.35 us
  loops' own time: 17.5 us -> 0 us
  local copies, waits for them, and re-layouts: 26.5 us -> 12.1 us
    reduce_scatter x1 -> x0, waiting for transfers between devices: 107 us -> none  [per_device(): shares = lax.psum_scatter(parts, 'dp', scatter_dimension=2, tiled=True)]
    pallas_call x0 -> x3, Pallas kernels: none -> 82.9 us  [the longest x1 73.2 us: call_stats(): pl.pallas_call(stats_kernel, name='stats', out_shape=(jax.ShapeDtypeStruc...]
    psum x1, blocking collectives: 145 us -> 83.4 us  [per_device(): update_norm = lax.psum(jnp.sum(sq), ('dp', 'mp'))]
    all_to_all x1, waiting for transfers between devices: 75.8 us -> 16.9 us  [per_device(): lax.all_to_all(sending, 'dp', split_axis=1, concat_axis=1, tiled=True)]
    all_to_all x1 -> x0, blocking collectives: 21.7 us -> none  [per_device(): lax.all_to_all(sending, 'dp', split_axis=1, concat_axis=1, tiled=True)]
    dot_general x6 -> x1, matrix products: 21.5 us -> 1.35 us  [per_device(): jnp.einsum('djk,jdrc->krc', chooser.astype(BF16), gotten, preferred_eleme...]
    another operation x2 -> x0, loops' own time: 17.5 us -> none  [per_device(): lax.cond(targets[position] >= 0, refresh_pair, keep_pair, (new_accum[posi...]
    ppermute x0 -> x8, waiting for transfers between devices: none -> 14.8 us  [permute(): return lax.ppermute(x, 'dp', pairs)]
  transfers between devices with their start and end apart: 3 -> 10, of which waited for: 3 -> 5; matrix products, arithmetic and copies ran while one was open for 1% -> 0% of each run, Pallas kernels for 0% -> 0%
where the time goes in v1:
time: 279 us; the launch traced here: 278 us
  blocking collectives  83.4 us (30%)
  Pallas kernels  82.9 us (30%)
  waiting for transfers between devices  71.6 us (26%)
  between operations  14.8 us (5%)
  local copies, waits for them, and re-layouts  12.1 us (4%)
  starting transfers between devices  11.1 us (4%)
    psum x1, blocking collectives, per_device(): update_norm = lax.psum(jnp.sum(sq), ('dp', 'mp'))  83.4 us
    pallas_call x1, Pallas kernels, call_stats(): pl.pallas_call(stats_kernel, name='stats', out_shape=(jax.ShapeDtypeStruc...  73.2 us
    all_gather x1, waiting for transfers between devices, per_device(): update = lax.all_gather(picked, 'dp', axis=1, tiled=True)  40 us
    all_to_all x1, waiting for transfers between devices, per_device(): lax.all_to_all(sending, 'dp', split_axis=1, concat_axis=1, tiled=True)  16.9 us
    ppermute x8, waiting for transfers between devices, permute(): return lax.ppermute(x, 'dp', pairs)  14.8 us
    unnamed x11, local copies, waits for them, and re-layouts  9.4 us
    all_to_all x1, starting transfers between devices, per_device(): lax.all_to_all(sending, 'dp', split_axis=1, concat_axis=1, tiled=True)  6.52 us
    pallas_call x1, Pallas kernels, call_roots(): pl.pallas_call(roots_kernel, name='roots', out_shape=(jax.ShapeDtypeStruc...  5.8 us
  transfers between devices with their start and end apart: 10, of which 5 were waited for; matrix products, arithmetic and copies ran while one was open for 0% of the time, Pallas kernels for 0%

profile of v1, /device:TPU:1, one launch (start us, length us, event | category | flops | bytes accessed | tf_op | source)
XLA Modules:
  0.0 278.2 jit_solution(970025683485554152)
XLA Ops:
  7.2 0.7 pad.4.rf_ref
  7.8 2.2 copy-done
  10.0 1.6 copy-done.2
  11.6 73.2 %stats.1 = (f32[2,4,4,5,64,128]{5,4,3,2,1,0:T(8,128)S(1)}, f32[4,4,64,128]{3,2,1,0:T(8,128)S(1)}, f32[2,512,512]{2,1,0:T(8,128)S(1)}, s32[8,128]{1,0:T(8,128)S(1)}) custom-call(bf16[4,512,512]{2,1,0:T(8,128)(2,1)S(1)} %bitcast.19, s32[8,128]{1,0:T(8,128)S(1)} %pad.4.rf_ref, f32[2,2,512,512]{3,2,1,0:T(8,128)S(1)} %bitcast.17), custom_call_target="tpu_custom_call" | custom-call | tf_op jit(solution)/shard_map/stats/pallas_call | solution.py:241
  84.9 2.3 copy-done.4
  87.2 5.8 %roots.1 = (f32[2,2,512,512]{3,2,1,0:T(8,128)}, f32[2,512,512]{2,1,0:T(8,128)S(1)}, f32[2,512,512]{2,1,0:T(8,128)S(1)}) custom-call(s32[1,4]{1,0:T(1,128)S(1)} %copy-done.3, s32[8,128]{1,0:T(8,128)S(1)} %pad.4.rf_ref, s32[8,128]{1,0:T(8,128)S(1)} %get-tuple-element.13.prf_ref, f32[4,2,10,128,128]{4,3,2,1,0:T(8,128)} %bitcast.21, ...), custom_call_target="tpu_custom_call" | custom-call | flops 20000000000 | bytes 20971520 | tf_op jit(solution)/shard_map/roots/pallas_call | solution.py:443
  93.0 0.2 collective-permute-start
  93.2 2.0 collective-permute-start.1
  95.2 0.0 collective-permute-start.2
  95.2 0.5 collective-permute-start.3
  95.8 0.9 collective-permute-start.4
  96.6 10.3 %collective-permute-done.1.rest_1_ = f32[4,4,64,128]{3,2,1,0:T(8,128)S(1)} collective-permute-done((f32[4,4,64,128]{3,2,1,0:T(8,128)S(1)}, f32[4,4,64,128]{3,2,1,0:T(8,128)S(1)}, u32[]{:S(2)}, u32[]{:S(2)}) %collective-permute-start.1) | collective-permute-done | bytes 524320 | tf_op jit(solution)/shard_map/ppermute | solution.py:571
  106.9 0.0 collective-permute-start.5
  107.0 0.0 collective-permute-done.2.rest_2_
  107.0 0.5 collective-permute-start.6
  107.5 2.9 %collective-permute-done.3.rest_3_ = f32[4,4,64,128]{3,2,1,0:T(8,128)S(1)} collective-permute-done((f32[4,4,64,128]{3,2,1,0:T(8,128)S(1)}, f32[4,4,64,128]{3,2,1,0:T(8,128)S(1)}, u32[]{:S(2)}, u32[]{:S(2)}) %collective-permute-start.3) | collective-permute-done | bytes 524320 | tf_op jit(solution)/shard_map/ppermute | solution.py:571
  110.4 0.4 collective-permute-start.7
  110.8 0.0 collective-permute-done.6.rest_6_
  110.8 1.5 collective-permute-done.7.rest_7_
  112.4 0.0 collective-permute-done.r_ref
  112.4 3.9 %product.1 = (f32[2,2,512,512]{3,2,1,0:T(8,128)}, f32[8,128]{1,0:T(8,128)S(1)}, f32[2,512,512]{2,1,0:T(8,128)S(1)}) custom-call(s32[1,4]{1,0:T(1,128)S(1)} %copy-done.3, s32[8,128]{1,0:T(8,128)S(1)} %pad.4.rf_ref, f32[2,512,512]{2,1,0:T(8,128)S(1)} %get-tuple-element.17.l_ref, f32[2,512,512]{2,1,0:T(8,128)S(1)} %collective-permute-done.r_ref, ...), custom_call_target="tpu_custom_call" | custom-call | tf_op jit(solution)/shard_map/product/pallas_call | solution.py:543
  116.2 0.6 reduce_sum.9
  116.8 83.4 %psum.7 = f32[]{:T(128)} all-reduce(f32[]{:T(128)} %reduce_sum.9), channel_id=1, replica_groups=mesh['dp'=32,'mp'=4] {'dp','mp'}, use_global_device_ids=true, to_apply=%region_1.2 | all-reduce | flops 1 | bytes 8 | tf_op jit(solution)/shard_map/psum | solution.py:595
  200.9 0.3 multiply_convert_fusion
  201.2 2.1 copy.10
  203.3 6.5 %all-to-all-start = ((bf16[2,32,16,512]{3,0,2,1:T(2,128)(2,1)}), bf16[2,32,16,512]{3,0,2,1:T(2,128)(2,1)S(1)}, u32[]{:S(2)}, u32[]{:S(2)}) async-start(bf16[2,32,16,512]{3,0,2,1:T(2,128)(2,1)} %copy.10), calls=%async_computation | async-start | bytes 2097152 | tf_op jit(solution)/shard_map/all_to_all | solution.py:601
  209.8 0.0 all-gather.2.cloned.1.call-start
  209.8 16.9 %all-to-all-done = bf16[2,32,16,512]{3,0,2,1:T(2,128)(2,1)S(1)} async-done(((bf16[2,32,16,512]{3,0,2,1:T(2,128)(2,1)}), bf16[2,32,16,512]{3,0,2,1:T(2,128)(2,1)S(1)}, u32[]{:S(2)}, u32[]{:S(2)}) %all-to-all-start) | async-done | bytes 1048608 | tf_op jit(solution)/shard_map/all_to_all | solution.py:601
  226.7 1.4 fusion
  228.0 0.0 all-gather.2.cloned.1.call-update
  228.1 40.0 %all-gather.2.cloned.1.call-done = bf16[4,512,512]{2,0,1:T(4,128)(2,1)} async-done(((bf16[4,16,512]{2,0,1:T(4,128)(2,1)}), bf16[4,512,512]{2,0,1:T(4,128)(2,1)}) %all-gather.2.cloned.1.call-update) | async-done | bytes 2097168 | tf_op jit(solution)/shard_map/all_gather | solution.py:605
  268.1 3.3 %copy.12 = bf16[4,512,512]{2,1,0:T(8,128)(2,1)} copy(bf16[4,512,512]{2,0,1:T(4,128)(2,1)} %all-gather.2.cloned.1.call-done) | data formatting | bytes 4194304
  (10 shorter events, 0.0 us)
Async XLA Ops:
  7.8 2.2 copy-start
  10.0 1.6 copy-start.2
  11.6 75.6 %copy-start.1 = (f32[1,1,2,2,512,512]{5,4,3,2,1,0:T(8,128)S(1)}, f32[1,1,2,2,512,512]{5,4,3,2,1,0:T(8,128)}, u32[]{:S(2)}) copy-start(f32[1,1,2,2,512,512]{5,4,3,2,1,0:T(8,128)} %param.8) | copy-start | bytes 12582916
  11.6 75.6 %copy-start.3 = (s32[1,4]{1,0:T(1,128)S(1)}, s32[1,4]{1,0:T(1,128)}, u32[]{:S(2)}) copy-start(s32[1,4]{1,0:T(1,128)} %owner_ref.3) | copy-start | bytes 52
  84.9 2.3 copy-start.4
  93.0 19.4 %collective-permute-start = (f32[2,512,512]{2,1,0:T(8,128)S(1)}, f32[2,512,512]{2,1,0:T(8,128)S(1)}, u32[]{:S(2)}, u32[]{:S(2)}) collective-permute-start(f32[2,512,512]{2,1,0:T(8,128)S(1)} %get-tuple-element.18), channel_id=1, source_target_pairs={{0,4},{4,0},{8,12},{12,8},{16,20},{20,16},{24,28},{28,24},{32,36},... | collective-permute-start | bytes 6291464 | tf_op jit(solution)/shard_map/ppermute | solution.py:571
  93.2 13.7 %collective-permute-start.1 = (f32[4,4,64,128]{3,2,1,0:T(8,128)S(1)}, f32[4,4,64,128]{3,2,1,0:T(8,128)S(1)}, u32[]{:S(2)}, u32[]{:S(2)}) collective-permute-start(f32[4,4,64,128]{3,2,1,0:T(8,128)S(1)} %get-tuple-element.19.rest_0_), channel_id=1, source_target_pairs={{0,24},{4,100},{8,0},{12,108},{16,8},{20,116},{24,16},{28,124},{32... | collective-permute-start | bytes 1572872 | tf_op jit(solution)/shard_map/ppermute | solution.py:571
  95.2 11.8 %collective-permute-start.2 = (f32[4,4,64,128]{3,2,1,0:T(8,128)S(1)}, f32[4,4,64,128]{3,2,1,0:T(8,128)S(1)}, u32[]{:S(2)}, u32[]{:S(2)}) collective-permute-start(f32[4,4,64,128]{3,2,1,0:T(8,128)S(1)} %get-tuple-element.19.rest_0_), channel_id=1, source_target_pairs={{0,16},{4,68},{8,24},{12,76},{16,0},{20,84},{24,8},{28,92},{32,48}... | collective-permute-start | bytes 1572872 | tf_op jit(solution)/shard_map/ppermute | solution.py:571
  95.2 15.2 %collective-permute-start.3 = (f32[4,4,64,128]{3,2,1,0:T(8,128)S(1)}, f32[4,4,64,128]{3,2,1,0:T(8,128)S(1)}, u32[]{:S(2)}, u32[]{:S(2)}) collective-permute-start(f32[4,4,64,128]{3,2,1,0:T(8,128)S(1)} %get-tuple-element.19.rest_0_), channel_id=1, source_target_pairs={{0,8},{4,36},{8,16},{12,44},{16,24},{20,52},{24,0},{28,60},{32,40}... | collective-permute-start | bytes 1572872 | tf_op jit(solution)/shard_map/ppermute | solution.py:571
  95.8 15.0 %collective-permute-start.4 = (f32[4,4,64,128]{3,2,1,0:T(8,128)S(1)}, f32[4,4,64,128]{3,2,1,0:T(8,128)S(1)}, u32[]{:S(2)}, u32[]{:S(2)}) collective-permute-start(f32[4,4,64,128]{3,2,1,0:T(8,128)S(1)} %get-tuple-element.19.rest_0_), channel_id=1, source_target_pairs={{0,4},{4,0},{8,12},{12,8},{16,20},{20,16},{24,28},{28,24},{32,36},... | collective-permute-start | bytes 1572872 | tf_op jit(solution)/shard_map/ppermute | solution.py:571
  106.9 3.9 %collective-permute-start.5 = (f32[4,4,64,128]{3,2,1,0:T(8,128)S(1)}, f32[4,4,64,128]{3,2,1,0:T(8,128)S(1)}, u32[]{:S(2)}, u32[]{:S(2)}) collective-permute-start(f32[4,4,64,128]{3,2,1,0:T(8,128)S(1)} %collective-permute-done.1.rest_1_), channel_id=1, source_target_pairs={{0,4},{4,0},{8,12},{12,8},{16,20},{20,16},{24,28},{28,24},{32,36},... | collective-permute-start | bytes 1572872 | tf_op jit(solution)/shard_map/ppermute | solution.py:571
  107.0 3.9 %collective-permute-start.6 = (f32[4,4,64,128]{3,2,1,0:T(8,128)S(1)}, f32[4,4,64,128]{3,2,1,0:T(8,128)S(1)}, u32[]{:S(2)}, u32[]{:S(2)}) collective-permute-start(f32[4,4,64,128]{3,2,1,0:T(8,128)S(1)} %collective-permute-done.2.rest_2_), channel_id=1, source_target_pairs={{0,4},{4,0},{8,12},{12,8},{16,20},{20,16},{24,28},{28,24},{32,36},... | collective-permute-start | bytes 1572872 | tf_op jit(solution)/shard_map/ppermute | solution.py:571
  110.4 2.0 collective-permute-start.7
  203.3 23.4 %all-to-all-start = ((bf16[2,32,16,512]{3,0,2,1:T(2,128)(2,1)}), bf16[2,32,16,512]{3,0,2,1:T(2,128)(2,1)S(1)}, u32[]{:S(2)}, u32[]{:S(2)}) async-start(bf16[2,32,16,512]{3,0,2,1:T(2,128)(2,1)} %copy.10), calls=%async_computation | async-start | bytes 2097152 | tf_op jit(solution)/shard_map/all_to_all | solution.py:601
  209.8 58.3 %all-gather.2.cloned.1.call-start = ((), (), s32[]{:S(2)}) async-start(), calls=%async_computation.1 | async-start | bytes 2162688 | tf_op jit(solution)/shard_map/all_gather | solution.py:605
Sparse Core Ops, SparseCore 0:
  228.2 39.8 all-gather.1

commit v2 on v1

--- a/solution.py
+++ b/solution.py
@@ -563,6 +563,222 @@
     )(owner, refresh, lroot, rroot, old, *pieces)
 
 
+def tail_kernel(
+    n_mp, owner_ref, p_ref, sq_ref, up_ref,
+    na, nb, pbuf, sb, r1, r2, f3,
+    s_a, q_a, s_b, q_b, s_p, q_p, s_own, s1, q1, s2, q2, s3, q3, s4, q4, sd, qd, sl,
+):
+    y, z, c = coords()
+    x = lax.axis_index("mp")
+    pos1 = z + c * (y - z)
+    pos2 = y + c * (z - y)
+    plane = y * 4 + z
+    pair = x * 2 + c
+
+    def dev1(p):
+        return at(y + c * (p - y), p + c * (z - p), c)
+
+    def dev2(p):
+        return at(p + c * (y - p), z + c * (p - z), c)
+
+    mate = at(y, z, 1 - c)
+
+    def in_plane(n):
+        return {"dp": n * 2 + c}
+
+    def in_pair(n):
+        return {"dp": plane * 2 + n % 2, "mp": n // 2}
+
+    barrier = pltpu.get_barrier_semaphore()
+    for o in range(1, 16):
+        pl.semaphore_signal(barrier, inc=1, device_id=in_plane((plane + o) % 16), device_id_type=MESH)
+    for o in range(1, 2 * n_mp):
+        pl.semaphore_signal(barrier, inc=1, device_id=in_pair((pair + o) % (2 * n_mp)), device_id_type=MESH)
+    pl.semaphore_wait(barrier, 15 + 2 * n_mp - 1)
+
+    def rcopy(src, dst, ss, rs, device):
+        return pltpu.make_async_remote_copy(
+            src_ref=src, dst_ref=dst, send_sem=ss, recv_sem=rs, device_id=device, device_id_type=MESH
+        )
+
+    na[plane] = sq_ref[...]
+
+    def ca(o):
+        return rcopy(na.at[plane], na.at[plane], s_a.at[o - 1], q_a.at[o - 1], in_plane((plane - o + 16) % 16))
+
+    for o in range(1, 16):
+        ca(o).start()
+
+    def halves(j):
+        return rcopy(
+            p_ref.at[j, pl.ds((1 - c) * 256, 256)], pbuf.at[SLOTS + j], s_p.at[j], q_p.at[j], mate
+        )
+
+    def own(j):
+        return pltpu.make_async_copy(p_ref.at[j, pl.ds(c * 256, 256)], pbuf.at[j], s_own.at[j])
+
+    for j in range(SLOTS):
+        halves(j).start()
+        own(j).start()
+    pbuf[2 * SLOTS] = jnp.zeros((256, BS), F32)
+    for o in range(1, 16):
+        ca(o).wait_recv()
+    total = na[0]
+    for n in range(1, 16):
+        total = total + na[n]
+    nb[pair] = total
+
+    def cb(o):
+        n = 2 * n_mp
+        return rcopy(nb.at[pair], nb.at[pair], s_b.at[o - 1], q_b.at[o - 1], in_pair((pair - o + n) % n))
+
+    for o in range(1, 2 * n_mp):
+        cb(o).start()
+    for j in range(SLOTS):
+        halves(j).wait_recv()
+        own(j).wait()
+    for o in range(1, 2 * n_mp):
+        cb(o).wait_recv()
+    total = nb[0]
+    for n in range(1, 2 * n_mp):
+        total = total + nb[n]
+    square = jnp.sum(jnp.sum(total, axis=0, keepdims=True), axis=1, keepdims=True)
+    ratio = 1.0 / jnp.sqrt(square / float(KB * n_mp * BS * BS) + epsilon)
+
+    base = (plane * 2 + c) * SLOTS
+    mate_base = (plane * 2 + 1 - c) * SLOTS
+    index = []
+    for k in range(KB):
+        place = owner_ref[0, k]
+        n = jnp.int32(2 * SLOTS)
+        for j in range(SLOTS):
+            n = n + (j - 2 * SLOTS) * (place == base + j).astype(jnp.int32)
+            n = n + (j - SLOTS) * (place == mate_base + j).astype(jnp.int32)
+        index.append(n)
+
+    def c1(p, o):
+        return rcopy(sb.at[p], r1.at[o - 1], s1.at[o - 1], q1.at[o - 1], dev1(p))
+
+    @pl.loop(0, 4)
+    def _(i):
+        p = (pos1 + jnp.where(i == 0, 2, jnp.where(i == 1, 1, jnp.where(i == 2, 3, 0)))) % 4
+        o = (pos1 - p + 4) % 4
+        for k in range(KB):
+            for q in range(4):
+                block = pbuf[index[k], pl.ds(p * 64 + q * 16, 16), :]
+                sb[p, q, k] = (ratio * block).astype(BF16)
+
+        @pl.when(i < 3)
+        def _():
+            c1(p, o).start()
+
+    def c2(q):
+        o = (pos2 - q + 4) % 4
+        return rcopy(sb.at[pos1, q], r2.at[o - 1], s2.at[o - 1], q2.at[o - 1], dev2(q))
+
+    for o in (1, 2, 3):
+        c1(pos1, o).wait_recv()
+
+    @pl.loop(1, 5)
+    def _(k):
+        q = (pos2 + k) % 4
+        sb[pos1, q] = (sb[pos1, q] + r1[0, q]) + (r1[1, q] + r1[2, q])
+
+        @pl.when(k < 4)
+        def _():
+            c2(q).start()
+
+    for o in (1, 2, 3):
+        c2((pos2 + o) % 4).wait_recv()
+    f3[pos2] = (sb[pos1, pos2] + r2[0]) + (r2[1] + r2[2])
+
+    def c3(o):
+        return rcopy(f3.at[pos2], f3.at[pos2], s3.at[o - 1], q3.at[o - 1], dev2((pos2 - o + 4) % 4))
+
+    def out(core, p, q):
+        return up_ref.at[:, pl.ds(core * 256 + p * 64 + q * 16, 16), :]
+
+    def c4(o, q):
+        return rcopy(
+            f3.at[q], out(c, pos1, q), s4.at[o - 1, q], q4.at[o - 1, q], dev1((pos1 - o + 4) % 4)
+        )
+
+    def cd_own(q):
+        return rcopy(f3.at[q], out(c, pos1, q), sd.at[0, q], qd.at[0, q], mate)
+
+    def cd(o, q):
+        p = (pos1 + o) % 4
+        return rcopy(out(c, p, q), out(c, p, q), sd.at[o, q], qd.at[o, q], mate)
+
+    def keep(q):
+        return pltpu.make_async_copy(f3.at[q], out(c, pos1, q), sl.at[q])
+
+    for o in (2, 1, 3):
+        c3(o).start()
+    for k in (0, 1, 3, 2):
+        q = (pos2 + k) % 4
+        if k:
+            rcopy(f3.at[pos2], f3.at[q], s3.at[k - 1], q3.at[k - 1], dev2(q)).wait_recv()
+        for o in (2, 1, 3):
+            c4(o, q).start()
+        cd_own(q).start()
+        keep(q).start()
+    for o in (1, 3, 2):
+        for k in (0, 1, 3, 2):
+            q = (pos2 + k) % 4
+            p = (pos1 + o) % 4
+            rcopy(f3.at[q], out(c, p, q), s4.at[o - 1, q], q4.at[o - 1, q], dev1(p)).wait_recv()
+            cd(o, q).start()
+
+    for o in range(1, 16):
+        ca(o).wait_send()
+    for o in range(1, 2 * n_mp):
+        cb(o).wait_send()
+    for j in range(SLOTS):
+        halves(j).wait_send()
+    for k in range(1, 4):
+        p = (pos1 + k) % 4
+        c1(p, (pos1 - p + 4) % 4).wait_send()
+        c2((pos2 + k) % 4).wait_send()
+        c3(k).wait_send()
+    for q in range(4):
+        keep(q).wait()
+        for o in (1, 2, 3):
+            c4(o, q).wait_send()
+            cd(o, q).wait_send()
+        cd_own(q).wait_send()
+        for o in range(4):
+            p = (pos2 + o) % 4
+            rcopy(f3.at[q], out(1 - c, p, q), sd.at[o, q], qd.at[o, q], mate).wait_recv()
+
+
+def call_tail(owner, product, sq, n_mp):
+    dma = pltpu.SemaphoreType.DMA
+    return pl.pallas_call(
+        functools.partial(tail_kernel, n_mp),
+        name="tail",
+        out_shape=jax.ShapeDtypeStruct((KB, BS, BS), BF16),
+        in_specs=[pl.BlockSpec(memory_space=pltpu.SMEM)] + [pl.BlockSpec(memory_space=pltpu.VMEM)] * 2,
+        out_specs=pl.BlockSpec(memory_space=pl.ANY),
+        scratch_shapes=[
+            pltpu.VMEM((16, 8, TL), F32),
+            pltpu.VMEM((2 * n_mp, 8, TL), F32),
+            pltpu.VMEM((2 * SLOTS + 1, 256, BS), F32),
+            pltpu.VMEM((4, 4, KB, 16, BS), BF16),
+            pltpu.VMEM((3, 4, KB, 16, BS), BF16),
+            pltpu.VMEM((3, KB, 16, BS), BF16),
+            pltpu.VMEM((4, KB, 16, BS), BF16),
+            dma((15,)), dma((15,)), dma((2 * n_mp - 1,)), dma((2 * n_mp - 1,)),
+            dma((SLOTS,)), dma((SLOTS,)), dma((SLOTS,)),
+            dma((3,)), dma((3,)), dma((3,)), dma((3,)), dma((3,)), dma((3,)),
+            dma((3, 4)), dma((3, 4)), dma((4, 4)), dma((4, 4)), dma((4,)),
+        ],
+        compiler_params=pltpu.CompilerParams(
+            collective_id=2, has_side_effects=True, vmem_limit_bytes=40 << 20
+        ),
+    )(owner, product, sq)
+
+
 def permute(x, n, place):
     pairs = []
     for d in range(n):
@@ -578,7 +794,6 @@
 def per_device(grads, block_owner, refresh_to, accum_old, roots_old):
     n_dp = lax.axis_size("dp")
     n_mp = lax.axis_size("mp")
-    my_index = lax.axis_index("dp")
     acc, old = accum_old[0, 0], roots_old[0, 0]
     refresh = jnp.pad(refresh_to[0], ((0, 7), (0, TL - SLOTS)))
     stats, gq, pacc, prefresh = call_stats(grads[0], refresh, acc)
@@ -592,17 +807,7 @@
     rroot = permute(rroot, n_dp, swap)
     roots, sq, product = call_product(block_owner, refresh, lroot, rroot, old, pieces)
 
-    update_norm = lax.psum(jnp.sum(sq), ("dp", "mp"))
-    ratio = 1.0 / jnp.sqrt(update_norm / float(KB * n_mp * BS * BS) + epsilon)
-    scaled = (ratio * product).astype(BF16)
-    places = jnp.arange(n_dp * SLOTS, dtype=jnp.int32).reshape(n_dp, SLOTS)
-    chooser = places[:, :, None] == block_owner[0][None, None, :]
-    sending = scaled.reshape(SLOTS, n_dp, BS // n_dp, BS)
-    gotten = lax.all_to_all(sending, "dp", split_axis=1, concat_axis=1, tiled=True)
-    picked = jnp.einsum(
-        "djk,jdrc->krc", chooser.astype(BF16), gotten, preferred_element_type=F32
-    ).astype(BF16)
-    update = lax.all_gather(picked, "dp", axis=1, tiled=True)
+    update = call_tail(block_owner, product, sq, n_mp)
     return (new_accum[None, None], roots[None, None], update)
 
 

time: 279 us -> 170 us (0.61)
  blocking collectives: 83.4 us -> 0 us
  waiting for transfers between devices: 71.6 us -> 5.21 us
  Pallas kernels: 82.9 us -> 134 us
  between operations: 14.8 us -> 0.69 us
  starting transfers between devices: 11.1 us -> 21.8 us
  local copies, waits for them, and re-layouts: 12.1 us -> 8.07 us
    psum x1 -> x0, blocking collectives: 83.4 us -> none  [per_device(): update_norm = lax.psum(jnp.sum(sq), ('dp', 'mp'))]
    pallas_call x0 -> x1, Pallas kernels: none -> 51.5 us  [call_tail(): pl.pallas_call(functools.partial(tail_kernel, n_mp), name='tail', out_sha...]
    all_gather x1 -> x0, waiting for transfers between devices: 40 us -> none  [per_device(): update = lax.all_gather(picked, 'dp', axis=1, tiled=True)]
    ppermute x8, starting transfers between devices: 4.58 us -> 21.8 us  [permute(): return lax.ppermute(x, 'dp', pairs)]
    all_to_all x1 -> x0, waiting for transfers between devices: 16.9 us -> none  [per_device(): lax.all_to_all(sending, 'dp', split_axis=1, concat_axis=1, tiled=True)]
    ppermute x8, waiting for transfers between devices: 14.8 us -> 5.21 us  [permute(): return lax.ppermute(x, 'dp', pairs)]
    all_to_all x1 -> x0, starting transfers between devices: 6.52 us -> none  [per_device(): lax.all_to_all(sending, 'dp', split_axis=1, concat_axis=1, tiled=True)]
  transfers between devices with their start and end apart: 10 -> 8, of which waited for: 5 -> 2; matrix products, arithmetic and copies ran while one was open for 0% -> 0% of each run, Pallas kernels for 0% -> 0%
where the time goes in v2:
time: 170 us
  Pallas kernels  134 us (79%)
  starting transfers between devices  21.8 us (13%)
  local copies, waits for them, and re-layouts  8.07 us (5%)
  waiting for transfers between devices  5.21 us (3%)
    pallas_call x1, Pallas kernels, call_stats(): pl.pallas_call(stats_kernel, name='stats', out_shape=(jax.ShapeDtypeStruc...  73.2 us
    pallas_call x1, Pallas kernels, call_tail(): pl.pallas_call(functools.partial(tail_kernel, n_mp), name='tail', out_sha...  51.5 us
    ppermute x8, starting transfers between devices, permute(): return lax.ppermute(x, 'dp', pairs)  21.8 us
    unnamed x11, local copies, waits for them, and re-layouts  7.41 us
    pallas_call x1, Pallas kernels, call_roots(): pl.pallas_call(roots_kernel, name='roots', out_shape=(jax.ShapeDtypeStruc...  5.8 us
    ppermute x8, waiting for transfers between devices, permute(): return lax.ppermute(x, 'dp', pairs)  5.21 us
    pallas_call x1, Pallas kernels, call_product(): pl.pallas_call(product_kernel, name='product', out_shape=(jax.ShapeDtypeS...  3.86 us
  transfers between devices with their start and end apart: 8, of which 2 were waited for; matrix products, arithmetic and copies ran while one was open for 0% of the time, Pallas kernels for 0%

profile of v2, /device:TPU:1, one launch (start us, length us, event | category | flops | bytes accessed | tf_op | source)
XLA Modules:
  0.0 170.1 jit_solution(7545552703089188186)
XLA Ops:
  0.6 0.7 pad.4.rf_ref
  1.3 0.0 copy-start
  1.3 2.2 %copy-done = f32[1,1,2,2,512,512]{5,4,3,2,1,0:T(8,128)S(1)} copy-done((f32[1,1,2,2,512,512]{5,4,3,2,1,0:T(8,128)S(1)}, f32[1,1,2,2,512,512]{5,4,3,2,1,0:T(8,128)}, u32[]{:S(2)}) %copy-start) | copy-done | bytes 4194328
  3.5 0.0 copy-start.2
  3.5 1.6 copy-done.2
  5.1 0.0 copy-start.1
  5.1 0.0 copy-start.3
  5.1 73.2 %stats.1 = (f32[2,4,4,5,64,128]{5,4,3,2,1,0:T(8,128)S(1)}, f32[4,4,64,128]{3,2,1,0:T(8,128)S(1)}, f32[2,512,512]{2,1,0:T(8,128)S(1)}, s32[8,128]{1,0:T(8,128)S(1)}) custom-call(bf16[4,512,512]{2,1,0:T(8,128)(2,1)S(1)} %bitcast.9, s32[8,128]{1,0:T(8,128)S(1)} %pad.4.rf_ref, f32[2,2,512,512]{3,2,1,0:T(8,128)S(1)} %bitcast.7), custom_call_target="tpu_custom_call" | custom-call | tf_op jit(solution)/shard_map/stats/pallas_call | solution.py:241
  78.3 0.0 copy-start.4
  78.3 2.3 %copy-done.4 = f32[2,4,4,5,64,128]{5,4,3,2,1,0:T(8,128)} copy-done((f32[2,4,4,5,64,128]{5,4,3,2,1,0:T(8,128)}, f32[2,4,4,5,64,128]{5,4,3,2,1,0:T(8,128)S(1)}, u32[]{:S(2)}) %copy-start.4) | copy-done | bytes 5242904
  80.6 0.0 copy-done.1
  80.6 0.0 copy-done.3
  80.6 5.8 %roots.1 = (f32[2,2,512,512]{3,2,1,0:T(8,128)}, f32[2,512,512]{2,1,0:T(8,128)S(1)}, f32[2,512,512]{2,1,0:T(8,128)S(1)}) custom-call(s32[1,4]{1,0:T(1,128)S(1)} %copy-done.3, s32[8,128]{1,0:T(8,128)S(1)} %pad.4.rf_ref, s32[8,128]{1,0:T(8,128)S(1)} %get-tuple-element.13.prf_ref, f32[4,2,10,128,128]{4,3,2,1,0:T(8,128)} %bitcast.10, ...), custom_call_target="tpu_custom_call" | custom-call | flops 20000000000 | bytes 20971520 | tf_op jit(solution)/shard_map/roots/pallas_call | solution.py:443
  86.4 0.2 collective-permute-start
  86.7 2.0 %collective-permute-start.1 = (f32[4,4,64,128]{3,2,1,0:T(8,128)S(1)}, f32[4,4,64,128]{3,2,1,0:T(8,128)S(1)}, u32[]{:S(2)}, u32[]{:S(2)}) collective-permute-start(f32[4,4,64,128]{3,2,1,0:T(8,128)S(1)} %get-tuple-element.19.rest_0_), channel_id=1, source_target_pairs={{0,24},{4,100},{8,0},{12,108},{16,8},{20,116},{24,16},{28,124},{32... | collective-permute-start | bytes 1572872 | tf_op jit(solution)/shard_map/ppermute | solution.py:787
  88.6 0.0 collective-permute-start.2
  88.7 0.5 collective-permute-start.3
  89.2 7.5 %collective-permute-start.4 = (f32[4,4,64,128]{3,2,1,0:T(8,128)S(1)}, f32[4,4,64,128]{3,2,1,0:T(8,128)S(1)}, u32[]{:S(2)}, u32[]{:S(2)}) collective-permute-start(f32[4,4,64,128]{3,2,1,0:T(8,128)S(1)} %get-tuple-element.19.rest_0_), channel_id=1, source_target_pairs={{0,4},{4,0},{8,12},{12,8},{16,20},{20,16},{24,28},{28,24},{32,36},... | collective-permute-start | bytes 1572872 | tf_op jit(solution)/shard_map/ppermute | solution.py:787
  96.7 3.7 %collective-permute-done.1.rest_1_ = f32[4,4,64,128]{3,2,1,0:T(8,128)S(1)} collective-permute-done((f32[4,4,64,128]{3,2,1,0:T(8,128)S(1)}, f32[4,4,64,128]{3,2,1,0:T(8,128)S(1)}, u32[]{:S(2)}, u32[]{:S(2)}) %collective-permute-start.1) | collective-permute-done | bytes 524320 | tf_op jit(solution)/shard_map/ppermute | solution.py:787
  100.4 7.8 %collective-permute-start.5 = (f32[4,4,64,128]{3,2,1,0:T(8,128)S(1)}, f32[4,4,64,128]{3,2,1,0:T(8,128)S(1)}, u32[]{:S(2)}, u32[]{:S(2)}) collective-permute-start(f32[4,4,64,128]{3,2,1,0:T(8,128)S(1)} %collective-permute-done.1.rest_1_), channel_id=1, source_target_pairs={{0,4},{4,0},{8,12},{12,8},{16,20},{20,16},{24,28},{28,24},{32,36},... | collective-permute-start | bytes 1572872 | tf_op jit(solution)/shard_map/ppermute | solution.py:787
  108.2 0.0 collective-permute-done.2.rest_2_
  108.2 0.0 collective-permute-start.6
  108.2 0.0 collective-permute-done.3.rest_3_
  108.2 3.7 %collective-permute-start.7 = (f32[4,4,64,128]{3,2,1,0:T(8,128)S(1)}, f32[4,4,64,128]{3,2,1,0:T(8,128)S(1)}, u32[]{:S(2)}, u32[]{:S(2)}) collective-permute-start(f32[4,4,64,128]{3,2,1,0:T(8,128)S(1)} %collective-permute-done.3.rest_3_), channel_id=1, source_target_pairs={{0,4},{4,0},{8,12},{12,8},{16,20},{20,16},{24,28},{28,24},{32,36},... | collective-permute-start | bytes 1572872 | tf_op jit(solution)/shard_map/ppermute | solution.py:787
  111.9 0.0 collective-permute-done.4.rest_4_
  111.9 0.0 collective-permute-done.5.rest_5_
  111.9 0.0 collective-permute-done.6.rest_6_
  111.9 1.5 collective-permute-done.7.rest_7_
  113.4 0.0 collective-permute-done.r_ref
  113.4 3.9 %product.1 = (f32[2,2,512,512]{3,2,1,0:T(8,128)}, f32[8,128]{1,0:T(8,128)S(1)}, f32[2,512,512]{2,1,0:T(8,128)S(1)}) custom-call(s32[1,4]{1,0:T(1,128)S(1)} %copy-done.3, s32[8,128]{1,0:T(8,128)S(1)} %pad.4.rf_ref, f32[2,512,512]{2,1,0:T(8,128)S(1)} %get-tuple-element.17.l_ref, f32[2,512,512]{2,1,0:T(8,128)S(1)} %collective-permute-done.r_ref, ...), custom_call_target="tpu_custom_call" | custom-call | tf_op jit(solution)/shard_map/product/pallas_call | solution.py:543
  117.3 51.5 %tail.1 = bf16[4,512,512]{2,1,0:T(8,128)(2,1)S(1)} custom-call(s32[1,4]{1,0:T(1,128)S(1)} %copy-done.3, f32[2,512,512]{2,1,0:T(8,128)S(1)} %get-tuple-element.21.p_ref, f32[8,128]{1,0:T(8,128)S(1)} %get-tuple-element.22.sq_ref), custom_call_target="tpu_custom_call" | custom-call | tf_op jit(solution)/shard_map/tail/pallas_call | solution.py:757
  168.8 1.3 copy.9
Async XLA Ops:
  1.3 2.2 %copy-start = (f32[1,1,2,2,512,512]{5,4,3,2,1,0:T(8,128)S(1)}, f32[1,1,2,2,512,512]{5,4,3,2,1,0:T(8,128)}, u32[]{:S(2)}) copy-start(f32[1,1,2,2,512,512]{5,4,3,2,1,0:T(8,128)} %param.8) | copy-start | bytes 12582916
  3.5 1.6 copy-start.2
  5.1 75.5 %copy-start.1 = (f32[1,1,2,2,512,512]{5,4,3,2,1,0:T(8,128)S(1)}, f32[1,1,2,2,512,512]{5,4,3,2,1,0:T(8,128)}, u32[]{:S(2)}) copy-start(f32[1,1,2,2,512,512]{5,4,3,2,1,0:T(8,128)} %param.8) | copy-start | bytes 12582916
  5.1 75.5 %copy-start.3 = (s32[1,4]{1,0:T(1,128)S(1)}, s32[1,4]{1,0:T(1,128)}, u32[]{:S(2)}) copy-start(s32[1,4]{1,0:T(1,128)} %owner_ref.5) | copy-start | bytes 52
  78.3 2.3 %copy-start.4 = (f32[2,4,4,5,64,128]{5,4,3,2,1,0:T(8,128)}, f32[2,4,4,5,64,128]{5,4,3,2,1,0:T(8,128)S(1)}, u32[]{:S(2)}) copy-start(f32[2,4,4,5,64,128]{5,4,3,2,1,0:T(8,128)S(1)} %get-tuple-element.14) | copy-start | bytes 15728644
  86.4 27.0 %collective-permute-start = (f32[2,512,512]{2,1,0:T(8,128)S(1)}, f32[2,512,512]{2,1,0:T(8,128)S(1)}, u32[]{:S(2)}, u32[]{:S(2)}) collective-permute-start(f32[2,512,512]{2,1,0:T(8,128)S(1)} %get-tuple-element.18), channel_id=1, source_target_pairs={{0,4},{4,0},{8,12},{12,8},{16,20},{20,16},{24,28},{28,24},{32,36},... | collective-permute-start | bytes 6291464 | tf_op jit(solution)/shard_map/ppermute | solution.py:787
  86.7 13.7 %collective-permute-start.1 = (f32[4,4,64,128]{3,2,1,0:T(8,128)S(1)}, f32[4,4,64,128]{3,2,1,0:T(8,128)S(1)}, u32[]{:S(2)}, u32[]{:S(2)}) collective-permute-start(f32[4,4,64,128]{3,2,1,0:T(8,128)S(1)} %get-tuple-element.19.rest_0_), channel_id=1, source_target_pairs={{0,24},{4,100},{8,0},{12,108},{16,8},{20,116},{24,16},{28,124},{32... | collective-permute-start | bytes 1572872 | tf_op jit(solution)/shard_map/ppermute | solution.py:787
  88.6 19.5 %collective-permute-start.2 = (f32[4,4,64,128]{3,2,1,0:T(8,128)S(1)}, f32[4,4,64,128]{3,2,1,0:T(8,128)S(1)}, u32[]{:S(2)}, u32[]{:S(2)}) collective-permute-start(f32[4,4,64,128]{3,2,1,0:T(8,128)S(1)} %get-tuple-element.19.rest_0_), channel_id=1, source_target_pairs={{0,16},{4,68},{8,24},{12,76},{16,0},{20,84},{24,8},{28,92},{32,48}... | collective-permute-start | bytes 1572872 | tf_op jit(solution)/shard_map/ppermute | solution.py:787
  88.7 19.5 %collective-permute-start.3 = (f32[4,4,64,128]{3,2,1,0:T(8,128)S(1)}, f32[4,4,64,128]{3,2,1,0:T(8,128)S(1)}, u32[]{:S(2)}, u32[]{:S(2)}) collective-permute-start(f32[4,4,64,128]{3,2,1,0:T(8,128)S(1)} %get-tuple-element.19.rest_0_), channel_id=1, source_target_pairs={{0,8},{4,36},{8,16},{12,44},{16,24},{20,52},{24,0},{28,60},{32,40}... | collective-permute-start | bytes 1572872 | tf_op jit(solution)/shard_map/ppermute | solution.py:787
  89.2 22.6 %collective-permute-start.4 = (f32[4,4,64,128]{3,2,1,0:T(8,128)S(1)}, f32[4,4,64,128]{3,2,1,0:T(8,128)S(1)}, u32[]{:S(2)}, u32[]{:S(2)}) collective-permute-start(f32[4,4,64,128]{3,2,1,0:T(8,128)S(1)} %get-tuple-element.19.rest_0_), channel_id=1, source_target_pairs={{0,4},{4,0},{8,12},{12,8},{16,20},{20,16},{24,28},{28,24},{32,36},... | collective-permute-start | bytes 1572872 | tf_op jit(solution)/shard_map/ppermute | solution.py:787
  100.4 11.5 %collective-permute-start.5 = (f32[4,4,64,128]{3,2,1,0:T(8,128)S(1)}, f32[4,4,64,128]{3,2,1,0:T(8,128)S(1)}, u32[]{:S(2)}, u32[]{:S(2)}) collective-permute-start(f32[4,4,64,128]{3,2,1,0:T(8,128)S(1)} %collective-permute-done.1.rest_1_), channel_id=1, source_target_pairs={{0,4},{4,0},{8,12},{12,8},{16,20},{20,16},{24,28},{28,24},{32,36},... | collective-permute-start | bytes 1572872 | tf_op jit(solution)/shard_map/ppermute | solution.py:787
  108.2 3.7 %collective-permute-start.6 = (f32[4,4,64,128]{3,2,1,0:T(8,128)S(1)}, f32[4,4,64,128]{3,2,1,0:T(8,128)S(1)}, u32[]{:S(2)}, u32[]{:S(2)}) collective-permute-start(f32[4,4,64,128]{3,2,1,0:T(8,128)S(1)} %collective-permute-done.2.rest_2_), channel_id=1, source_target_pairs={{0,4},{4,0},{8,12},{12,8},{16,20},{20,16},{24,28},{28,24},{32,36},... | collective-permute-start | bytes 1572872 | tf_op jit(solution)/shard_map/ppermute | solution.py:787
  108.2 5.2 %collective-permute-start.7 = (f32[4,4,64,128]{3,2,1,0:T(8,128)S(1)}, f32[4,4,64,128]{3,2,1,0:T(8,128)S(1)}, u32[]{:S(2)}, u32[]{:S(2)}) collective-permute-start(f32[4,4,64,128]{3,2,1,0:T(8,128)S(1)} %collective-permute-done.3.rest_3_), channel_id=1, source_target_pairs={{0,4},{4,0},{8,12},{12,8},{16,20},{20,16},{24,28},{28,24},{32,36},... | collective-permute-start | bytes 1572872 | tf_op jit(solution)/shard_map/ppermute | solution.py:787

commit v3 on v2

v3 whole, which is shorter than its diff:
```python
import functools

import jax
import jax.numpy as jnp
from jax import lax
from jax.experimental import pallas as pl
from jax.experimental.pallas import tpu as pltpu
from jax.sharding import PartitionSpec as P

MESH = pl.DeviceIdType.MESH
F32 = jnp.float32
BF16 = jnp.bfloat16

BS = 512
KB = 4
SLOTS = 2
TL = 128
TILES = [(a, b) for a in range(4) for b in range(a, 4)]
NT = len(TILES)
SP = 5
GP = 4
decay_rate = 0.8
epsilon = 1e-06


def coords():
    d = lax.axis_index("dp")
    return d // 8, (d // 2) % 4, d % 2


def at(y, z, c):
    return {"dp": (y * 4 + z) * 2 + c}


def dot_nt(a, b):
    return lax.dot_general(a, b, (((1,), (1,)), ((), ())), preferred_element_type=F32)


def dot_tn(a, b):
    return lax.dot_general(a, b, (((0,), (0,)), ((), ())), preferred_element_type=F32)


def dot_nn(a, b):
    return lax.dot_general(a, b, (((1,), (0,)), ((), ())), preferred_element_type=F32)


W0 = 25 / 16
W1 = -5 / 16 - 3125 / 4096
W2 = 3125 / 4096
W3 = -1250 / 4096
W4 = 250 / 4096
W5 = -25 / 4096
W6 = 1 / 4096


def split(x):
    hi = x.astype(BF16)
    return hi, (x - hi.astype(F32)).astype(BF16)


def dot3(ah, al, bh, bl):
    return dot_nn(ah, bh) + (dot_nn(ah, bl) + dot_nn(al, bh))


def find_slot(owner_ref, place):
    block = jnp.int32(0)
    alive = jnp.int32(0)
    for k in range(KB):
        hit = (owner_ref[0, k] == place).astype(jnp.int32)
        block = jnp.where(hit == 1, k, block)
        alive = jnp.maximum(alive, hit)
    return block, alive


def inverse_root(a_ref, store, bufs):
    mf, m2f, nf, zf, mh, ml, ah, al, bh, bl, ch, cl = bufs
    a = a_ref[...]
    square = jnp.sum(a * a, axis=0, keepdims=True)
    mean = jnp.sum(square, axis=1, keepdims=True) * (1.0 / (BS * BS))
    scale = BS * jnp.sqrt(mean + epsilon)
    inverse = 1.0 / scale
    outer = 1.0 / jnp.sqrt(jnp.sqrt(scale))
    lo, up = slice(0, 256), slice(256, 512)

    def put(f, h, l, v, rows, cols):
        for x, r, k in ((v, rows, cols),) if rows is cols else ((v, rows, cols), (v.T, cols, rows)):
            hi = x.astype(BF16)
            h[r, k] = hi
            if f is not None:
                f[r, k] = x
            if l is not None:
                l[r, k] = (x - hi.astype(F32)).astype(BF16)

    def multiply(lh, ll, rh, rl, then):
        for rows, cols in ((lo, lo), (lo, up), (up, up)):
            if rl is None:
                q = dot_nn(lh[rows, :], rh[:, cols])
            else:
                q = dot3(lh[rows, :], ll[rows, :], rh[:, cols], rl[:, cols])
            then(q, rows, cols)

    for rows in (lo, up):
        x = a_ref[rows, :] * inverse
        mf[rows, :] = x
        mh[rows, :], ml[rows, :] = split(x)
    multiply(mh, ml, mh, ml, lambda q, r, k: put(m2f, ah, al, q, r, k))

    def third(q, r, k):
        m, m2 = mf[r, k], m2f[r, k]
        nf[r, k] = W1 * m + W2 * m2 + W3 * q
        put(None, bh, None, q, r, k)
        put(None, ch, None, W4 * m + W5 * m2 + W6 * q, r, k)

    multiply(ah, al, mh, ml, third)
    multiply(ch, None, bh, None, lambda q, r, k: put(nf, ah, al, nf[r, k] + q, r, k))
    multiply(ah, al, mh, ml, lambda q, r, k: put(zf, ch, cl, W0 * mf[r, k] + q, r, k))
    multiply(ah, al, ah, al, lambda q, r, k: put(m2f, bh, bl, (2 * W0) * nf[r, k] + q, r, k))
    multiply(bh, bl, bh, bl, lambda q, r, k: put(None, ah, al, (2 * W0 * W0) * m2f[r, k] + q, r, k))

    def last(q, r, k):
        x = 1.25 * nf[r, k] - (0.25 * W0**4) * zf[r, k] - 0.25 * q
        if r is k:
            rows = lax.broadcasted_iota(jnp.int32, (256, 256), 0)
            cols = lax.broadcasted_iota(jnp.int32, (256, 256), 1)
            x = x + jnp.where(rows == cols, F32(1.25 * W0), F32(0.0))
        x = outer * x
        store(r, k, x)
        if r is not k:
            store(k, r, x.T)

    multiply(ah, al, ch, cl, last)


class Spread:
    def __init__(self, st, r1, r2, every, sems, place):
        self.st, self.r1, self.r2, self.all = st, r1, r2, every
        self.s1, self.q1, self.s2, self.q2, self.s3, self.q3, self.s4, self.q4, self.sd, self.qd = sems
        self.c, self.pos1, self.pos2, self.dev1, self.dev2, self.mate = place

    def c1(self, p, q):
        o = (self.pos1 - p + 4) % 4 - 1
        return rcopy(
            self.st.at[p, q], self.r1.at[o, q], self.s1.at[o, q], self.q1.at[o, q], self.dev1(p)
        )

    def c2(self, q):
        o = (self.pos2 - q + 4) % 4 - 1
        return rcopy(self.st.at[self.pos1, q], self.r2.at[o], self.s2.at[o], self.q2.at[o], self.dev2(q))

    def c3(self, o, q, device):
        ref = self.all.at[self.c, self.pos1, q]
        return rcopy(ref, ref, self.s3.at[o - 1], self.q3.at[o - 1], device)

    def c4(self, o, p, q, device):
        ref = self.all.at[self.c, p, q]
        return rcopy(ref, ref, self.s4.at[o - 1, q], self.q4.at[o - 1, q], device)

    def cd(self, core, p, q):
        ref = self.all.at[core, p, q]
        return rcopy(ref, ref, self.sd.at[p, q], self.qd.at[p, q], self.mate)

    def send1(self, p):
        for k in range(4):
            self.c1(p, (self.pos2 + 1 + k) % 4).start()

    def add1(self):
        for k in range(1, 5):
            q = (self.pos2 + k) % 4
            for o in (1, 2, 3):
                self.c1((self.pos1 + o) % 4, q).wait_recv()
            self.st[self.pos1, q] = (self.st[self.pos1, q] + self.r1[0, q]) + (self.r1[1, q] + self.r1[2, q])
            if k < 4:
                self.c2(q).start()

    def add2(self):
        for o in (1, 2, 3):
            self.c2((self.pos2 + o) % 4).wait_recv()
        self.all[self.c, self.pos1, self.pos2] = (self.st[self.pos1, self.pos2] + self.r2[0]) + (
            self.r2[1] + self.r2[2]
        )
        for o in (2, 1, 3):
            self.c3(o, self.pos2, self.dev2((self.pos2 - o + 4) % 4)).start()

    def gather2(self):
        for k in (0, 1, 3, 2):
            q = (self.pos2 + k) % 4
            if k:
                self.c3(k, q, self.dev2(q)).wait_recv()
            for o in (2, 1, 3):
                self.c4(o, self.pos1, q, self.dev1((self.pos1 - o + 4) % 4)).start()
            self.cd(self.c, self.pos1, q).start()

    def gather1(self):
        for o in (1, 3, 2):
            p = (self.pos1 + o) % 4
            for k in (0, 1, 3, 2):
                q = (self.pos2 + k) % 4
                self.c4(o, p, q, self.dev1(p)).wait_recv()
                self.cd(self.c, p, q).start()

    def from_mate(self):
        for p in range(4):
            for q in range(4):
                self.cd(1 - self.c, p, q).wait_recv()

    def sent(self):
        for o in (1, 2, 3):
            for q in range(4):
                self.c1((self.pos1 + o) % 4, q).wait_send()
                self.c4(o, self.pos1, q, self.dev1((self.pos1 - o + 4) % 4)).wait_send()
            self.c2((self.pos2 + o) % 4).wait_send()
            self.c3(o, self.pos2, self.dev2((self.pos2 - o + 4) % 4)).wait_send()
        for p in range(4):
            for q in range(4):
                self.cd(self.c, p, q).wait_send()

    @staticmethod
    def sems():
        dma = pltpu.SemaphoreType.DMA
        return [dma((3, 4)), dma((3, 4)), dma((3,)), dma((3,)), dma((3,)), dma((3,)),
                dma((3, 4)), dma((3, 4)), dma((4, 4)), dma((4, 4))]


def rcopy(src, dst, ss, rs, device):
    return pltpu.make_async_remote_copy(
        src_ref=src, dst_ref=dst, send_sem=ss, recv_sem=rs, device_id=device, device_id_type=MESH
    )


def main_kernel(owner_ref, g_ref, acc_ref, new_ref, gs_ref, lroot_ref, rroot_ref, *scratch):
    (praw, sts, sr1, sr2, sall, stg, gr1, gr2, pacc, am, rsend), scratch = scratch[:11], scratch[11:]
    bufs, scratch = scratch[:12], scratch[12:]
    ssem, gsem, (s_raw, s_acc, s_old, s_root) = scratch[:10], scratch[10:20], scratch[20:]
    y, z, c = coords()
    pos1 = z + c * (y - z)
    pos2 = y + c * (z - y)

    def dev1(p):
        return at(y + c * (p - y), p + c * (z - p), c)

    def dev2(p):
        return at(p + c * (y - p), z + c * (p - z), c)

    mate = at(y, z, 1 - c)
    place = (c, pos1, pos2, dev1, dev2, mate)
    stat = Spread(sts, sr1, sr2, sall, ssem, place)
    gsum = Spread(stg, gr1, gr2, gs_ref, gsem, place)

    barrier = pltpu.get_barrier_semaphore()
    for o in (1, 2, 3):
        pl.semaphore_signal(barrier, inc=1, device_id=dev1((pos1 + o) % 4), device_id_type=MESH)
        pl.semaphore_signal(barrier, inc=1, device_id=dev2((pos2 + o) % 4), device_id_type=MESH)
    pl.semaphore_signal(barrier, inc=1, device_id=mate, device_id_type=MESH)
    pl.semaphore_wait(barrier, 7)

    raw = rcopy(g_ref.at[pl.ds(2 * (1 - c), 2)], praw, s_raw.at[0], s_raw.at[1], mate)
    raw.start()
    accs = [rcopy(acc_ref.at[j, 1], pacc.at[j], s_acc.at[0, j], s_acc.at[1, j], mate) for j in range(SLOTS)]
    olds = [pltpu.make_async_copy(acc_ref.at[j], new_ref.at[j], s_old.at[j]) for j in range(SLOTS)]
    raw.wait()
    for a in accs + olds:
        a.start()

    def put(p, a, b, block):
        t = TILES.index((a, b))
        for half in range(2):
            h = 2 * t + half
            sts[p, h // SP, h % SP] = block[half * 64:(half + 1) * 64]

    def quadrants(p, quad):
        x = quad(0, 0)
        put(p, 0, 0, x[:128, :128])
        put(p, 0, 1, x[:128, 128:])
        put(p, 1, 1, x[128:, 128:])
        x = quad(0, 1)
        put(p, 0, 2, x[:128, :128])
        put(p, 0, 3, x[:128, 128:])
        put(p, 1, 2, x[128:, :128])
        put(p, 1, 3, x[128:, 128:])
        x = quad(1, 1)
        put(p, 2, 2, x[:128, :128])
        put(p, 2, 3, x[:128, 128:])
        put(p, 3, 3, x[128:, 128:])

    @pl.loop(0, 4)
    def _(i):
        p = (pos1 + jnp.where(i == 0, 2, jnp.where(i == 1, 1, jnp.where(i == 2, 3, 0)))) % 4
        blk = p // 2

        @pl.when(p % 2 == 0)
        def _():
            quadrants(
                p,
                lambda a, b: dot_nt(
                    g_ref[2 * c + blk, a * 256:(a + 1) * 256, :], g_ref[2 * c + blk, b * 256:(b + 1) * 256, :]
                )
                + dot_nt(praw[blk, a * 256:(a + 1) * 256, :], praw[blk, b * 256:(b + 1) * 256, :]),
            )

        @pl.when(p % 2 == 1)
        def _():
            quadrants(
                p,
                lambda a, b: dot_tn(
                    g_ref[2 * c + blk, :, a * 256:(a + 1) * 256], g_ref[2 * c + blk, :, b * 256:(b + 1) * 256]
                )
                + dot_tn(praw[blk, :, a * 256:(a + 1) * 256], praw[blk, :, b * 256:(b + 1) * 256]),
            )

        @pl.when(i < 3)
        def _():
            stat.send1(p)

    @pl.loop(0, 4)
    def _(i):
        p = (pos1 + jnp.where(i == 0, 2, jnp.where(i == 1, 1, jnp.where(i == 2, 3, 0)))) % 4
        for q in range(4):
            rows = pl.ds((p % 2) * 256 + q * 64, 64)
            total = g_ref[2 * c + p // 2, rows, :].astype(F32) + praw[p // 2, rows, :].astype(F32)
            for k in range(GP):
                stg[p, q, k] = total[:, k * 128:(k + 1) * 128]

        @pl.when(i < 3)
        def _():
            gsum.send1(p)

    stat.add1()
    stat.add2()
    stat.gather2()
    gsum.add1()
    stat.gather1()
    gsum.add2()
    for a in accs:
        a.wait()
    for a in olds:
        a.wait()
    stat.from_mate()

    d = lax.axis_index("dp")
    other = d + 1 - 2 * c

    def blend(dst, src, blk, alive, lr):
        keep = jnp.where(alive == 1, F32(decay_rate), F32(1.0))
        take = jnp.where(alive == 1, F32((1.0 - decay_rate) / 16384.0), F32(0.0))
        for t, (a, b) in enumerate(TILES):
            for half in range(2):
                h = 2 * t + half
                fresh = take * sall[blk // 2, 2 * (blk % 2) + lr, h // SP, h % SP]
                ra, rb = pl.ds(a * TL + half * 64, 64), pl.ds(b * TL, TL)
                dst[ra, rb] = keep * src[ra, rb] + fresh
                if a != b:
                    dst[rb, ra] = keep * src[rb, ra] + fresh.T

    def root(j):
        return rcopy(rsend.at[j], rroot_ref.at[j], s_root.at[0, j], s_root.at[1, j], mate)

    @pl.loop(0, 4)
    def _(t):
        j = t % 2

        @pl.when(t < 2)
        def _():
            blk, _ = find_slot(owner_ref, other * SLOTS + j)
            blend(am, pacc.at[j], blk, jnp.int32(1), 1)

        @pl.when(t >= 2)
        def _():
            blk, alive = find_slot(owner_ref, d * SLOTS + j)
            blend(new_ref.at[j, 0], new_ref.at[j, 0], blk, alive, 0)
            blend(new_ref.at[j, 1], new_ref.at[j, 1], blk, alive, 1)
            am[...] = new_ref[j, 0]

        def store(rows, cols, x):
            @pl.when(t < 2)
            def _():
                rsend[j, rows, cols] = x

            @pl.when(t >= 2)
            def _():
                lroot_ref[j, rows, cols] = x

        inverse_root(am, store, bufs)

        @pl.when(t < 2)
        def _():
            root(j).start()

        @pl.when(t == 0)
        def _():
            gsum.gather2()

        @pl.when(t == 2)
        def _():
            gsum.gather1()

    for j in range(SLOTS):
        root(j).wait()
    gsum.from_mate()
    stat.sent()
    gsum.sent()


def call_main(owner, grads, acc):
    dma = pltpu.SemaphoreType.DMA
    vmem = pl.BlockSpec(memory_space=pltpu.VMEM)
    square = lambda n, dt: pltpu.VMEM(n + (BS, BS), dt)
    return pl.pallas_call(
        main_kernel,
        name="main",
        out_shape=(
            jax.ShapeDtypeStruct((SLOTS, 2, BS, BS), F32),
            jax.ShapeDtypeStruct((2, 4, 4, GP, 64, TL), F32),
            jax.ShapeDtypeStruct((SLOTS, BS, BS), F32),
            jax.ShapeDtypeStruct((SLOTS, BS, BS), F32),
        ),
        in_specs=[pl.BlockSpec(memory_space=pltpu.SMEM), vmem, pl.BlockSpec(memory_space=pl.ANY)],
        out_specs=(vmem,) * 4,
        scratch_shapes=[
            square((2,), BF16),
            pltpu.VMEM((4, 4, SP, 64, TL), F32),
            pltpu.VMEM((3, 4, SP, 64, TL), F32),
            pltpu.VMEM((3, SP, 64, TL), F32),
            pltpu.VMEM((2, 4, 4, SP, 64, TL), F32),
            pltpu.VMEM((4, 4, GP, 64, TL), F32),
            pltpu.VMEM((3, 4, GP, 64, TL), F32),
            pltpu.VMEM((3, GP, 64, TL), F32),
            square((SLOTS,), F32),
            square((), F32),
            square((SLOTS,), F32),
        ]
        + [square((), F32)] * 4 + [square((), BF16)] * 8
        + Spread.sems() + Spread.sems()
        + [dma((2,)), dma((2, SLOTS)), dma((SLOTS,)), dma((2, SLOTS))],
        compiler_params=pltpu.CompilerParams(
            collective_id=1, has_side_effects=True, vmem_limit_bytes=44 << 20
        ),
    )(owner, grads, acc)


def product_kernel(
    owner_ref, rf_ref, new_ref, gs_ref, l_ref, r_ref, old_ref,
    accum_ref, roots_ref, sq_ref, p_ref,
    flag, buf, gh, gl, sem,
):
    d = lax.axis_index("dp")
    accum = pltpu.make_async_copy(new_ref, accum_ref, sem.at[4])
    accum.start()
    for j in range(SLOTS):
        blk, alive = find_slot(owner_ref, d * SLOTS + j)
        fresh = alive * (rf_ref[0, j] >= 0).astype(jnp.int32)
        flag[0, j], flag[1, j], flag[2, j] = blk, alive, fresh
        for i, ref in enumerate((l_ref, r_ref)):
            @pl.when(fresh == 1)
            def _():
                pltpu.make_async_copy(ref.at[j], buf.at[j, i], sem.at[2 * j + i]).start()

            @pl.when(fresh == 0)
            def _():
                pltpu.make_async_copy(old_ref.at[j, i], buf.at[j, i], sem.at[2 * j + i]).start()
    sq_ref[...] = jnp.zeros_like(sq_ref)
    outs = []
    for j in range(SLOTS):
        for i in range(2):
            pltpu.make_async_copy(old_ref.at[j, i], buf.at[j, i], sem.at[2 * j + i]).wait()
        outs.append(pltpu.make_async_copy(buf.at[j], roots_ref.at[j], sem.at[5 + j]))
        outs[-1].start()

    @pl.loop(0, SLOTS)
    def _(j):
        @pl.when(flag[1, j] == 1)
        def _():
            blk = flag[0, j]
            for h in range(2):
                for q in range(4):
                    for k in range(4):
                        rows, cols = pl.ds(h * 256 + q * 64, 64), pl.ds(k * TL, TL)
                        gh[0, rows, cols], gl[0, rows, cols] = split(
                            gs_ref[blk // 2, 2 * (blk % 2) + h, q, k]
                        )
            gh[1], gl[1] = split(buf[j, 1])

            @pl.loop(0, 2)
            def _(h):
                rows = pl.ds(pl.multiple_of(h * 256, 256), 256)
                ah, al = split(buf[j, 0, rows, :])
                t = dot3(ah, al, gh[0], gl[0])
                th, tl = split(t)
                x = dot3(th, tl, gh[1], gl[1])
                p_ref[j, rows, :] = x
                part = jnp.sum((x * x).reshape(32, 8, BS), axis=0)
                sq_ref[...] += (part[:, :128] + part[:, 128:256]) + (part[:, 256:384] + part[:, 384:])

        @pl.when(flag[1, j] == 0)
        def _():
            p_ref[j] = jnp.zeros((BS, BS), F32)

    accum.wait()
    for o in outs:
        o.wait()


def call_product(owner, refresh, new, gs, lroot, rroot, old):
    anywhere = pl.BlockSpec(memory_space=pl.ANY)
    smem = pl.BlockSpec(memory_space=pltpu.SMEM)
    vmem = pl.BlockSpec(memory_space=pltpu.VMEM)
    return pl.pallas_call(
        product_kernel,
        name="product",
        out_shape=(
            jax.ShapeDtypeStruct((SLOTS, 2, BS, BS), F32),
            jax.ShapeDtypeStruct((SLOTS, 2, BS, BS), F32),
            jax.ShapeDtypeStruct((8, TL), F32),
            jax.ShapeDtypeStruct((SLOTS, BS, BS), F32),
        ),
        in_specs=[smem] * 2 + [vmem] * 4 + [anywhere],
        out_specs=(anywhere, anywhere, vmem, vmem),
        scratch_shapes=[
            pltpu.SMEM((3, SLOTS), jnp.int32),
            pltpu.VMEM((SLOTS, 2, BS, BS), F32),
            pltpu.VMEM((2, BS, BS), BF16),
            pltpu.VMEM((2, BS, BS), BF16),
            pltpu.SemaphoreType.DMA((7,)),
        ],
        compiler_params=pltpu.CompilerParams(vmem_limit_bytes=40 << 20),
    )(owner, refresh, new, gs, lroot, rroot, old)


def tail_kernel(
    n_mp, owner_ref, p_ref, sq_ref, up_ref,
    na, nb, pbuf, sb, r1, r2, f3,
    s_a, q_a, s_b, q_b, s_p, q_p, s_own, s1, q1, s2, q2, s3, q3, s4, q4, sd, qd, sl,
):
    y, z, c = coords()
    x = lax.axis_index("mp")
    pos1 = z + c * (y - z)
    pos2 = y + c * (z - y)
    plane = y * 4 + z
    pair = x * 2 + c

    def dev1(p):
        return at(y + c * (p - y), p + c * (z - p), c)

    def dev2(p):
        return at(p + c * (y - p), z + c * (p - z), c)

    mate = at(y, z, 1 - c)

    def in_plane(n):
        return {"dp": n * 2 + c}

    def in_pair(n):
        return {"dp": plane * 2 + n % 2, "mp": n // 2}

    barrier = pltpu.get_barrier_semaphore()
    for o in range(1, 16):
        pl.semaphore_signal(barrier, inc=1, device_id=in_plane((plane + o) % 16), device_id_type=MESH)
    for o in range(1, 2 * n_mp):
        pl.semaphore_signal(barrier, inc=1, device_id=in_pair((pair + o) % (2 * n_mp)), device_id_type=MESH)
    pl.semaphore_wait(barrier, 15 + 2 * n_mp - 1)

    na[plane] = sq_ref[...]

    def ca(o):
        return rcopy(na.at[plane], na.at[plane], s_a.at[o - 1], q_a.at[o - 1], in_plane((plane - o + 16) % 16))

    for o in range(1, 16):
        ca(o).start()

    def halves(j):
        return rcopy(
            p_ref.at[j, pl.ds((1 - c) * 256, 256)], pbuf.at[SLOTS + j], s_p.at[j], q_p.at[j], mate
        )

    def own(j):
        return pltpu.make_async_copy(p_ref.at[j, pl.ds(c * 256, 256)], pbuf.at[j], s_own.at[j])

    for j in range(SLOTS):
        halves(j).start()
        own(j).start()
    pbuf[2 * SLOTS] = jnp.zeros((256, BS), F32)
    for o in range(1, 16):
        ca(o).wait_recv()
    total = na[0]
    for n in range(1, 16):
        total = total + na[n]
    nb[pair] = total

    def cb(o):
        n = 2 * n_mp
        return rcopy(nb.at[pair], nb.at[pair], s_b.at[o - 1], q_b.at[o - 1], in_pair((pair - o + n) % n))

    for o in range(1, 2 * n_mp):
        cb(o).start()
    for j in range(SLOTS):
        halves(j).wait_recv()
        own(j).wait()
    for o in range(1, 2 * n_mp):
        cb(o).wait_recv()
    total = nb[0]
    for n in range(1, 2 * n_mp):
        total = total + nb[n]
    square = jnp.sum(jnp.sum(total, axis=0, keepdims=True), axis=1, keepdims=True)
    ratio = 1.0 / jnp.sqrt(square / float(KB * n_mp * BS * BS) + epsilon)

    base = (plane * 2 + c) * SLOTS
    mate_base = (plane * 2 + 1 - c) * SLOTS
    index = []
    for k in range(KB):
        place = owner_ref[0, k]
        n = jnp.int32(2 * SLOTS)
        for j in range(SLOTS):
            n = n + (j - 2 * SLOTS) * (place == base + j).astype(jnp.int32)
            n = n + (j - SLOTS) * (place == mate_base + j).astype(jnp.int32)
        index.append(n)

    def c1(p, o):
        return rcopy(sb.at[p], r1.at[o - 1], s1.at[o - 1], q1.at[o - 1], dev1(p))

    @pl.loop(0, 4)
    def _(i):
        p = (pos1 + jnp.where(i == 0, 2, jnp.where(i == 1, 1, jnp.where(i == 2, 3, 0)))) % 4
        o = (pos1 - p + 4) % 4
        for k in range(KB):
            for q in range(4):
                block = pbuf[index[k], pl.ds(p * 64 + q * 16, 16), :]
                sb[p, q, k] = (ratio * block).astype(BF16)

        @pl.when(i < 3)
        def _():
            c1(p, o).start()

    def c2(q):
        o = (pos2 - q + 4) % 4
        return rcopy(sb.at[pos1, q], r2.at[o - 1], s2.at[o - 1], q2.at[o - 1], dev2(q))

    for o in (1, 2, 3):
        c1(pos1, o).wait_recv()

    @pl.loop(1, 5)
    def _(k):
        q = (pos2 + k) % 4
        sb[pos1, q] = (sb[pos1, q] + r1[0, q]) + (r1[1, q] + r1[2, q])

        @pl.when(k < 4)
        def _():
            c2(q).start()

    for o in (1, 2, 3):
        c2((pos2 + o) % 4).wait_recv()
    f3[pos2] = (sb[pos1, pos2] + r2[0]) + (r2[1] + r2[2])

    def c3(o):
        return rcopy(f3.at[pos2], f3.at[pos2], s3.at[o - 1], q3.at[o - 1], dev2((pos2 - o + 4) % 4))

    def out(core, p, q):
        return up_ref.at[:, pl.ds(core * 256 + p * 64 + q * 16, 16), :]

    def c4(o, q):
        return rcopy(
            f3.at[q], out(c, pos1, q), s4.at[o - 1, q], q4.at[o - 1, q], dev1((pos1 - o + 4) % 4)
        )

    def cd_own(q):
        return rcopy(f3.at[q], out(c, pos1, q), sd.at[0, q], qd.at[0, q], mate)

    def cd(o, q):
        p = (pos1 + o) % 4
        return rcopy(out(c, p, q), out(c, p, q), sd.at[o, q], qd.at[o, q], mate)

    def keep(q):
        return pltpu.make_async_copy(f3.at[q], out(c, pos1, q), sl.at[q])

    for o in (2, 1, 3):
        c3(o).start()
    for k in (0, 1, 3, 2):
        q = (pos2 + k) % 4
        if k:
            rcopy(f3.at[pos2], f3.at[q], s3.at[k - 1], q3.at[k - 1], dev2(q)).wait_recv()
        for o in (2, 1, 3):
            c4(o, q).start()
        cd_own(q).start()
        keep(q).start()
    for o in (1, 3, 2):
        for k in (0, 1, 3, 2):
            q = (pos2 + k) % 4
            p = (pos1 + o) % 4
            rcopy(f3.at[q], out(c, p, q), s4.at[o - 1, q], q4.at[o - 1, q], dev1(p)).wait_recv()
            cd(o, q).start()

    for o in range(1, 16):
        ca(o).wait_send()
    for o in range(1, 2 * n_mp):
        cb(o).wait_send()
    for j in range(SLOTS):
        halves(j).wait_send()
    for k in range(1, 4):
        p = (pos1 + k) % 4
        c1(p, (pos1 - p + 4) % 4).wait_send()
        c2((pos2 + k) % 4).wait_send()
        c3(k).wait_send()
    for q in range(4):
        keep(q).wait()
        for o in (1, 2, 3):
            c4(o, q).wait_send()
            cd(o, q).wait_send()
        cd_own(q).wait_send()
        for o in range(4):
            p = (pos2 + o) % 4
            rcopy(f3.at[q], out(1 - c, p, q), sd.at[o, q], qd.at[o, q], mate).wait_recv()


def call_tail(owner, product, sq, n_mp):
    dma = pltpu.SemaphoreType.DMA
    return pl.pallas_call(
        functools.partial(tail_kernel, n_mp),
        name="tail",
        out_shape=jax.ShapeDtypeStruct((KB, BS, BS), BF16),
        in_specs=[pl.BlockSpec(memory_space=pltpu.SMEM)] + [pl.BlockSpec(memory_space=pltpu.VMEM)] * 2,
        out_specs=pl.BlockSpec(memory_space=pl.ANY),
        scratch_shapes=[
            pltpu.VMEM((16, 8, TL), F32),
            pltpu.VMEM((2 * n_mp, 8, TL), F32),
            pltpu.VMEM((2 * SLOTS + 1, 256, BS), F32),
            pltpu.VMEM((4, 4, KB, 16, BS), BF16),
            pltpu.VMEM((3, 4, KB, 16, BS), BF16),
            pltpu.VMEM((3, KB, 16, BS), BF16),
            pltpu.VMEM((4, KB, 16, BS), BF16),
            dma((15,)), dma((15,)), dma((2 * n_mp - 1,)), dma((2 * n_mp - 1,)),
            dma((SLOTS,)), dma((SLOTS,)), dma((SLOTS,)),
            dma((3,)), dma((3,)), dma((3,)), dma((3,)), dma((3,)), dma((3,)),
            dma((3, 4)), dma((3, 4)), dma((4, 4)), dma((4, 4)), dma((4,)),
        ],
        compiler_params=pltpu.CompilerParams(
            collective_id=2, has_side_effects=True, vmem_limit_bytes=40 << 20
        ),
    )(owner, product, sq)


def per_device(grads, block_owner, refresh_to, accum_old, roots_old):
    n_mp = lax.axis_size("mp")
    new, gs, lroot, rroot = call_main(block_owner, grads[0], accum_old[0, 0])
    new_accum, roots, sq, product = call_product(
        block_owner, refresh_to[0], new, gs, lroot, rroot, roots_old[0, 0]
    )
    update = call_tail(block_owner, product, sq, n_mp)
    return (new_accum[None, None], roots[None, None], update)


def solution(mesh):
    in_specs = (
        P("dp", "mp", None, None),
        P("mp", None),
        P("dp", "mp", None),
        P("dp", "mp", None, None, None, None),
        P("dp", "mp", None, None, None, None),
    )
    out_specs = (
        P("dp", "mp", None, None, None, None),
        P("dp", "mp", None, None, None, None),
        P("mp", None, None),
    )
    return jax.shard_map(
        per_device, mesh=mesh, in_specs=in_specs, out_specs=out_specs, check_vma=False
    )
```

time: 170 us -> 152 us (0.89)
  starting transfers between devices: 21.8 us -> 0 us
  Pallas kernels: 134 us -> 145 us
  waiting for transfers between devices: 5.21 us -> 0 us
  local copies, waits for them, and re-layouts: 8.07 us -> 5.76 us
    ppermute x8 -> x0, starting transfers between devices: 21.8 us -> none  [permute(): return lax.ppermute(x, 'dp', pairs)]
    pallas_call x2 -> x1, Pallas kernels: 79 us -> 96.2 us  [call_main(): pl.pallas_call(main_kernel, name='main', out_shape=(jax.ShapeDtypeStruct(...]
    pallas_call x1, Pallas kernels: 51.5 us -> 41.6 us  [call_tail(): pl.pallas_call(functools.partial(tail_kernel, n_mp), name='tail', out_sha...]
    ppermute x8 -> x0, waiting for transfers between devices: 5.21 us -> none  [permute(): return lax.ppermute(x, 'dp', pairs)]
    pallas_call x1, Pallas kernels: 3.86 us -> 7.34 us  [call_product(): pl.pallas_call(product_kernel, name='product', out_shape=(jax.ShapeDtypeS...]
  transfers between devices with their start and end apart: 8 -> 0, of which waited for: 2 -> 0; matrix products, arithmetic and copies ran while one was open for 0% -> 0% of each run, Pallas kernels for 0% -> 0%
where the time goes in v3:
time: 152 us
  Pallas kernels  145 us (95%)
  local copies, waits for them, and re-layouts  5.76 us (4%)
    pallas_call x1, Pallas kernels, call_main(): pl.pallas_call(main_kernel, name='main', out_shape=(jax.ShapeDtypeStruct(...  96.2 us
    pallas_call x1, Pallas kernels, call_tail(): pl.pallas_call(functools.partial(tail_kernel, n_mp), name='tail', out_sha...  41.6 us
    pallas_call x1, Pallas kernels, call_product(): pl.pallas_call(product_kernel, name='product', out_shape=(jax.ShapeDtypeS...  7.34 us
    unnamed x11, local copies, waits for them, and re-layouts  5.76 us

profile of v3, /device:TPU:1, one launch (start us, length us, event | category | flops | bytes accessed | tf_op | source)
XLA Modules:
  0.0 151.6 jit_solution(8356620864684528701)
XLA Ops:
  0.6 0.0 copy-start.3
  0.6 0.0 copy-start.4
  0.7 0.0 copy-start.1
  0.7 1.6 %copy-done.1 = bf16[1,4,512,512]{3,2,1,0:T(8,128)(2,1)S(1)} copy-done((bf16[1,4,512,512]{3,2,1,0:T(8,128)(2,1)S(1)}, bf16[1,4,512,512]{3,2,1,0:T(8,128)(2,1)}, u32[]{:S(2)}) %copy-start.1) | copy-done | bytes 2097176
  2.3 0.0 copy-start.2
  2.3 0.7 copy-done.2
  2.9 96.2 %main.1 = (f32[2,2,512,512]{3,2,1,0:T(8,128)}, f32[2,4,4,4,64,128]{5,4,3,2,1,0:T(8,128)}, f32[2,512,512]{2,1,0:T(8,128)S(1)}, f32[2,512,512]{2,1,0:T(8,128)S(1)}) custom-call(s32[1,4]{1,0:T(1,128)S(1)} %copy-done.2, bf16[4,512,512]{2,1,0:T(8,128)(2,1)S(1)} %bitcast.6, f32[2,2,512,512]{3,2,1,0:T(8,128)} %bitcast.8), custom_call_target="tpu_custom_call" | custom-call | tf_op jit(solution)/shard_map/main/pallas_call | solution.py:407
  99.1 0.0 copy-done.3
  99.2 0.0 copy-done.4
  99.2 0.0 copy-start
  99.2 2.2 %copy-done = f32[2,2,512,512]{3,2,1,0:T(8,128)S(1)} copy-done((f32[2,2,512,512]{3,2,1,0:T(8,128)S(1)}, f32[2,2,512,512]{3,2,1,0:T(8,128)}, u32[]{:S(2)}) %copy-start) | copy-done | bytes 4194328
  101.4 7.3 %product.1 = (f32[2,2,512,512]{3,2,1,0:T(8,128)}, f32[2,2,512,512]{3,2,1,0:T(8,128)}, f32[8,128]{1,0:T(8,128)S(1)}, f32[2,512,512]{2,1,0:T(8,128)S(1)}) custom-call(s32[1,4]{1,0:T(1,128)S(1)} %copy-done.3, s32[1,2]{1,0:T(1,128)S(1)} %bitcast.7, f32[2,2,512,512]{3,2,1,0:T(8,128)S(1)} %copy-done, f32[2,4,4,4,64,128]{5,4,3,2,1,0:T(8,128)} %get-tuple-element.12.gs_ref, ...), custom_call_target="tpu_custom_call" | custom-call | tf_op jit(solution)/shard_map/product/pallas_call | solution.py:506
  108.7 41.6 %tail.1 = bf16[4,512,512]{2,1,0:T(8,128)(2,1)S(1)} custom-call(s32[1,4]{1,0:T(1,128)S(1)} %copy-done.3, f32[2,512,512]{2,1,0:T(8,128)S(1)} %get-tuple-element.17.p_ref, f32[8,128]{1,0:T(8,128)S(1)} %get-tuple-element.18.sq_ref), custom_call_target="tpu_custom_call" | custom-call | tf_op jit(solution)/shard_map/tail/pallas_call | solution.py:714
  150.3 1.3 copy.9
Async XLA Ops:
  0.6 98.5 %copy-start.3 = (s32[1,4]{1,0:T(1,128)S(1)}, s32[1,4]{1,0:T(1,128)}, u32[]{:S(2)}) copy-start(s32[1,4]{1,0:T(1,128)} %owner_ref.5) | copy-start | bytes 52
  0.6 98.5 %copy-start.4 = (s32[1,1,2]{2,1,0:T(1,128)S(1)}, s32[1,1,2]{2,1,0:T(1,128)}, u32[]{:S(2)}) copy-start(s32[1,1,2]{2,1,0:T(1,128)} %param.7) | copy-start | bytes 28
  0.7 1.6 %copy-start.1 = (bf16[1,4,512,512]{3,2,1,0:T(8,128)(2,1)S(1)}, bf16[1,4,512,512]{3,2,1,0:T(8,128)(2,1)}, u32[]{:S(2)}) copy-start(bf16[1,4,512,512]{3,2,1,0:T(8,128)(2,1)} %param.5) | copy-start | bytes 6291460
  2.3 0.7 copy-start.2
  99.2 2.2 %copy-start = (f32[2,2,512,512]{3,2,1,0:T(8,128)S(1)}, f32[2,2,512,512]{3,2,1,0:T(8,128)}, u32[]{:S(2)}) copy-start(f32[2,2,512,512]{3,2,1,0:T(8,128)} %get-tuple-element.11.new_ref) | copy-start | bytes 12582916

commit v4 on v3

--- a/solution.py
+++ b/solution.py
@@ -228,9 +228,9 @@
 
 
 def main_kernel(owner_ref, g_ref, acc_ref, new_ref, gs_ref, lroot_ref, rroot_ref, *scratch):
-    (praw, sts, sr1, sr2, sall, stg, gr1, gr2, pacc, am, rsend), scratch = scratch[:11], scratch[11:]
+    (praw, accn, sts, sr1, sr2, sall, stg, gr1, gr2, pacc, am, rsend), scratch = scratch[:12], scratch[12:]
     bufs, scratch = scratch[:12], scratch[12:]
-    ssem, gsem, (s_raw, s_acc, s_old, s_root) = scratch[:10], scratch[10:20], scratch[20:]
+    ssem, gsem, (s_raw, s_acc, s_old, s_root, s_new) = scratch[:10], scratch[10:20], scratch[20:]
     y, z, c = coords()
     pos1 = z + c * (y - z)
     pos2 = y + c * (z - y)
@@ -246,6 +246,9 @@
     stat = Spread(sts, sr1, sr2, sall, ssem, place)
     gsum = Spread(stg, gr1, gr2, gs_ref, gsem, place)
 
+    olds = [pltpu.make_async_copy(acc_ref.at[j], accn.at[j], s_old.at[j]) for j in range(SLOTS)]
+    for a in olds:
+        a.start()
     barrier = pltpu.get_barrier_semaphore()
     for o in (1, 2, 3):
         pl.semaphore_signal(barrier, inc=1, device_id=dev1((pos1 + o) % 4), device_id_type=MESH)
@@ -256,9 +259,8 @@
     raw = rcopy(g_ref.at[pl.ds(2 * (1 - c), 2)], praw, s_raw.at[0], s_raw.at[1], mate)
     raw.start()
     accs = [rcopy(acc_ref.at[j, 1], pacc.at[j], s_acc.at[0, j], s_acc.at[1, j], mate) for j in range(SLOTS)]
-    olds = [pltpu.make_async_copy(acc_ref.at[j], new_ref.at[j], s_old.at[j]) for j in range(SLOTS)]
     raw.wait()
-    for a in accs + olds:
+    for a in accs:
         a.start()
 
     def put(p, a, b, block):
@@ -354,6 +356,9 @@
     def root(j):
         return rcopy(rsend.at[j], rroot_ref.at[j], s_root.at[0, j], s_root.at[1, j], mate)
 
+    def new(j):
+        return pltpu.make_async_copy(accn.at[j], new_ref.at[j], s_new.at[j])
+
     @pl.loop(0, 4)
     def _(t):
         j = t % 2
@@ -366,9 +371,10 @@
         @pl.when(t >= 2)
         def _():
             blk, alive = find_slot(owner_ref, d * SLOTS + j)
-            blend(new_ref.at[j, 0], new_ref.at[j, 0], blk, alive, 0)
-            blend(new_ref.at[j, 1], new_ref.at[j, 1], blk, alive, 1)
-            am[...] = new_ref[j, 0]
+            blend(accn.at[j, 0], accn.at[j, 0], blk, alive, 0)
+            blend(accn.at[j, 1], accn.at[j, 1], blk, alive, 1)
+            am[...] = accn[j, 0]
+            new(j).start()
 
         def store(rows, cols, x):
             @pl.when(t < 2)
@@ -395,6 +401,7 @@
 
     for j in range(SLOTS):
         root(j).wait()
+        new(j).wait()
     gsum.from_mate()
     stat.sent()
     gsum.sent()
@@ -403,6 +410,7 @@
 def call_main(owner, grads, acc):
     dma = pltpu.SemaphoreType.DMA
     vmem = pl.BlockSpec(memory_space=pltpu.VMEM)
+    hbm = pl.BlockSpec(memory_space=pltpu.HBM)
     square = lambda n, dt: pltpu.VMEM(n + (BS, BS), dt)
     return pl.pallas_call(
         main_kernel,
@@ -413,10 +421,11 @@
             jax.ShapeDtypeStruct((SLOTS, BS, BS), F32),
             jax.ShapeDtypeStruct((SLOTS, BS, BS), F32),
         ),
-        in_specs=[pl.BlockSpec(memory_space=pltpu.SMEM), vmem, pl.BlockSpec(memory_space=pl.ANY)],
-        out_specs=(vmem,) * 4,
+        in_specs=[pl.BlockSpec(memory_space=pltpu.SMEM), vmem, hbm],
+        out_specs=(hbm, vmem, vmem, vmem),
         scratch_shapes=[
             square((2,), BF16),
+            square((SLOTS, 2), F32),
             pltpu.VMEM((4, 4, SP, 64, TL), F32),
             pltpu.VMEM((3, 4, SP, 64, TL), F32),
             pltpu.VMEM((3, SP, 64, TL), F32),
@@ -430,9 +439,9 @@
         ]
         + [square((), F32)] * 4 + [square((), BF16)] * 8
         + Spread.sems() + Spread.sems()
-        + [dma((2,)), dma((2, SLOTS)), dma((SLOTS,)), dma((2, SLOTS))],
+        + [dma((2,)), dma((2, SLOTS)), dma((SLOTS,)), dma((2, SLOTS)), dma((SLOTS,))],
         compiler_params=pltpu.CompilerParams(
-            collective_id=1, has_side_effects=True, vmem_limit_bytes=44 << 20
+            collective_id=1, has_side_effects=True, vmem_limit_bytes=38 << 20
         ),
     )(owner, grads, acc)
 
@@ -440,33 +449,32 @@
 def product_kernel(
     owner_ref, rf_ref, new_ref, gs_ref, l_ref, r_ref, old_ref,
     accum_ref, roots_ref, sq_ref, p_ref,
-    flag, buf, gh, gl, sem,
+    flag, gh, gl, sem,
 ):
     d = lax.axis_index("dp")
-    accum = pltpu.make_async_copy(new_ref, accum_ref, sem.at[4])
+    accum = pltpu.make_async_copy(new_ref, accum_ref, sem.at[0])
     accum.start()
     for j in range(SLOTS):
         blk, alive = find_slot(owner_ref, d * SLOTS + j)
         fresh = alive * (rf_ref[0, j] >= 0).astype(jnp.int32)
         flag[0, j], flag[1, j], flag[2, j] = blk, alive, fresh
-        for i, ref in enumerate((l_ref, r_ref)):
-            @pl.when(fresh == 1)
-            def _():
-                pltpu.make_async_copy(ref.at[j], buf.at[j, i], sem.at[2 * j + i]).start()
-
-            @pl.when(fresh == 0)
-            def _():
-                pltpu.make_async_copy(old_ref.at[j, i], buf.at[j, i], sem.at[2 * j + i]).start()
+
+        @pl.when(fresh == 1)
+        def _():
+            for i, ref in enumerate((l_ref, r_ref)):
+                pltpu.make_async_copy(ref.at[j], roots_ref.at[j, i], sem.at[1 + 2 * j + i]).start()
+
+        @pl.when(fresh == 0)
+        def _():
+            for i in range(2):
+                pltpu.make_async_copy(old_ref.at[j, i], roots_ref.at[j, i], sem.at[1 + 2 * j + i]).start()
+
     sq_ref[...] = jnp.zeros_like(sq_ref)
-    outs = []
-    for j in range(SLOTS):
-        for i in range(2):
-            pltpu.make_async_copy(old_ref.at[j, i], buf.at[j, i], sem.at[2 * j + i]).wait()
-        outs.append(pltpu.make_async_copy(buf.at[j], roots_ref.at[j], sem.at[5 + j]))
-        outs[-1].start()
 
     @pl.loop(0, SLOTS)
     def _(j):
+        fresh = flag[2, j] == 1
+
         @pl.when(flag[1, j] == 1)
         def _():
             blk = flag[0, j]
@@ -477,12 +485,12 @@
                         gh[0, rows, cols], gl[0, rows, cols] = split(
                             gs_ref[blk // 2, 2 * (blk % 2) + h, q, k]
                         )
-            gh[1], gl[1] = split(buf[j, 1])
+            gh[1], gl[1] = split(jnp.where(fresh, r_ref[j], old_ref[j, 1]))
 
             @pl.loop(0, 2)
             def _(h):
                 rows = pl.ds(pl.multiple_of(h * 256, 256), 256)
-                ah, al = split(buf[j, 0, rows, :])
+                ah, al = split(jnp.where(fresh, l_ref[j, rows, :], old_ref[j, 0, rows, :]))
                 t = dot3(ah, al, gh[0], gl[0])
                 th, tl = split(t)
                 x = dot3(th, tl, gh[1], gl[1])
@@ -495,14 +503,16 @@
             p_ref[j] = jnp.zeros((BS, BS), F32)
 
     accum.wait()
-    for o in outs:
-        o.wait()
+    for j in range(SLOTS):
+        for i in range(2):
+            pltpu.make_async_copy(old_ref.at[j, i], roots_ref.at[j, i], sem.at[1 + 2 * j + i]).wait()
 
 
 def call_product(owner, refresh, new, gs, lroot, rroot, old):
     anywhere = pl.BlockSpec(memory_space=pl.ANY)
     smem = pl.BlockSpec(memory_space=pltpu.SMEM)
     vmem = pl.BlockSpec(memory_space=pltpu.VMEM)
+    hbm = pl.BlockSpec(memory_space=pltpu.HBM)
     return pl.pallas_call(
         product_kernel,
         name="product",
@@ -512,16 +522,15 @@
             jax.ShapeDtypeStruct((8, TL), F32),
             jax.ShapeDtypeStruct((SLOTS, BS, BS), F32),
         ),
-        in_specs=[smem] * 2 + [vmem] * 4 + [anywhere],
+        in_specs=[smem] * 2 + [hbm] + [vmem] * 4,
         out_specs=(anywhere, anywhere, vmem, vmem),
         scratch_shapes=[
             pltpu.SMEM((3, SLOTS), jnp.int32),
-            pltpu.VMEM((SLOTS, 2, BS, BS), F32),
             pltpu.VMEM((2, BS, BS), BF16),
             pltpu.VMEM((2, BS, BS), BF16),
-            pltpu.SemaphoreType.DMA((7,)),
+            pltpu.SemaphoreType.DMA((5,)),
         ],
-        compiler_params=pltpu.CompilerParams(vmem_limit_bytes=40 << 20),
+        compiler_params=pltpu.CompilerParams(vmem_limit_bytes=16 << 20),
     )(owner, refresh, new, gs, lroot, rroot, old)
 
 
@@ -731,7 +740,7 @@
             dma((3, 4)), dma((3, 4)), dma((4, 4)), dma((4, 4)), dma((4,)),
         ],
         compiler_params=pltpu.CompilerParams(
-            collective_id=2, has_side_effects=True, vmem_limit_bytes=40 << 20
+            collective_id=2, has_side_effects=True, vmem_limit_bytes=16 << 20
         ),
     )(owner, product, sq)
 

time: 152 us -> 143 us (0.941)
  Pallas kernels: 145 us -> 138 us
  local copies, waits for them, and re-layouts: 5.76 us -> 3.86 us
    pallas_call x1, Pallas kernels: 7.34 us -> 3.89 us  [call_product(): pl.pallas_call(product_kernel, name='product', out_shape=(jax.ShapeDtypeS...]
    pallas_call x1, Pallas kernels: 96.2 us -> 93.2 us  [call_main(): pl.pallas_call(main_kernel, name='main', out_shape=(jax.ShapeDtypeStruct(...]
    unnamed x11 -> x9, local copies, waits for them, and re-layouts: 5.76 us -> 3.86 us
where the time goes in v4:
time: 143 us
  Pallas kernels  138 us (97%)
  local copies, waits for them, and re-layouts  3.86 us (3%)
    pallas_call x1, Pallas kernels, call_main(): pl.pallas_call(main_kernel, name='main', out_shape=(jax.ShapeDtypeStruct(...  93.2 us
    pallas_call x1, Pallas kernels, call_tail(): pl.pallas_call(functools.partial(tail_kernel, n_mp), name='tail', out_sha...  41.1 us
    pallas_call x1, Pallas kernels, call_product(): pl.pallas_call(product_kernel, name='product', out_shape=(jax.ShapeDtypeS...  3.89 us
    unnamed x9, local copies, waits for them, and re-layouts  3.86 us

profile of v4, /device:TPU:1, one launch (start us, length us, event | category | flops | bytes accessed | tf_op | source)
XLA Modules:
  0.0 142.8 jit_solution(13548119240124323741)
XLA Ops:
  0.6 0.0 copy-start
  0.6 0.0 copy-start.1
  0.7 1.7 %copy-done.1 = bf16[1,4,512,512]{3,2,1,0:T(8,128)(2,1)S(1)} copy-done((bf16[1,4,512,512]{3,2,1,0:T(8,128)(2,1)S(1)}, bf16[1,4,512,512]{3,2,1,0:T(8,128)(2,1)}, u32[]{:S(2)}) %copy-start.1) | copy-done | bytes 2097176
  2.4 0.0 copy-start.2
  2.4 0.8 copy-done.2
  3.2 0.0 copy-start.3
  3.2 93.2 %main.1 = (f32[2,2,512,512]{3,2,1,0:T(8,128)S(1)}, f32[2,4,4,4,64,128]{5,4,3,2,1,0:T(8,128)S(1)}, f32[2,512,512]{2,1,0:T(8,128)S(1)}, f32[2,512,512]{2,1,0:T(8,128)S(1)}) custom-call(s32[1,4]{1,0:T(1,128)S(1)} %copy-done.2, bf16[4,512,512]{2,1,0:T(8,128)(2,1)S(1)} %bitcast.7, f32[2,2,512,512]{3,2,1,0:T(8,128)} %bitcast.9), custom_call_target="tpu_custom_call" | custom-call | tf_op jit(solution)/shard_map/main/pallas_call | solution.py:415
  96.4 0.0 copy-done
  96.4 0.0 copy-done.3
  96.4 3.9 %product.1 = (f32[2,2,512,512]{3,2,1,0:T(8,128)}, f32[2,2,512,512]{3,2,1,0:T(8,128)}, f32[8,128]{1,0:T(8,128)S(1)}, f32[2,512,512]{2,1,0:T(8,128)S(1)}) custom-call(s32[1,4]{1,0:T(1,128)S(1)} %copy-done.2, s32[1,2]{1,0:T(1,128)S(1)} %bitcast.8, f32[2,2,512,512]{3,2,1,0:T(8,128)S(1)} %get-tuple-element.11.new_ref, ...), custom_call_target="tpu_custom_call" | custom-call | tf_op jit(solution)/shard_map/product/pallas_call | solution.py:516
  100.3 41.1 %tail.1 = bf16[4,512,512]{2,1,0:T(8,128)(2,1)S(1)} custom-call(s32[1,4]{1,0:T(1,128)S(1)} %copy-done.2, f32[2,512,512]{2,1,0:T(8,128)S(1)} %get-tuple-element.17.p_ref, f32[8,128]{1,0:T(8,128)S(1)} %get-tuple-element.18.sq_ref), custom_call_target="tpu_custom_call" | custom-call | tf_op jit(solution)/shard_map/tail/pallas_call | solution.py:723
  141.4 1.3 copy.9
Async XLA Ops:
  0.6 95.7 %copy-start = (f32[1,1,2,2,512,512]{5,4,3,2,1,0:T(8,128)S(1)}, f32[1,1,2,2,512,512]{5,4,3,2,1,0:T(8,128)}, u32[]{:S(2)}) copy-start(f32[1,1,2,2,512,512]{5,4,3,2,1,0:T(8,128)} %param.9) | copy-start | bytes 12582916
  0.6 1.7 %copy-start.1 = (bf16[1,4,512,512]{3,2,1,0:T(8,128)(2,1)S(1)}, bf16[1,4,512,512]{3,2,1,0:T(8,128)(2,1)}, u32[]{:S(2)}) copy-start(bf16[1,4,512,512]{3,2,1,0:T(8,128)(2,1)} %param.5) | copy-start | bytes 6291460
  2.4 0.8 copy-start.2
  3.2 93.2 %copy-start.3 = (s32[1,1,2]{2,1,0:T(1,128)S(1)}, s32[1,1,2]{2,1,0:T(1,128)}, u32[]{:S(2)}) copy-start(s32[1,1,2]{2,1,0:T(1,128)} %param.7) | copy-start | bytes 28

commit v5 on v4

--- a/solution.py
+++ b/solution.py
@@ -221,6 +221,67 @@
                 dma((3, 4)), dma((3, 4)), dma((4, 4)), dma((4, 4))]
 
 
+ROWS = SP * 64
+GROUP = 16
+PACKED = ROWS + 32
+
+
+def pack(ref, x):
+    x = x.reshape(ROWS // GROUP, GROUP, TL)
+    top = jnp.maximum(jnp.max(jnp.abs(x), axis=1), 1e-30)
+    e = jnp.ceil(jnp.log2(top) * 64.0)
+    inverse = 32700.0 * jnp.exp2(e * (-1.0 / 64.0))
+    ref[0:ROWS, :] = jnp.round(x * inverse[:, None, :]).reshape(ROWS, TL).astype(jnp.int32).astype(jnp.int16)
+    e = jnp.concatenate([e, jnp.zeros((32 - ROWS // GROUP, TL), F32)], axis=0)
+    ref[ROWS:PACKED, :] = e.astype(jnp.int32).astype(jnp.int16)
+
+
+def unpack(ref):
+    e = ref[ROWS:PACKED, :].astype(jnp.int32).astype(F32)[: ROWS // GROUP]
+    scale = jnp.exp2(e * (1.0 / 64.0)) * (1.0 / 32700.0)
+    x = ref[0:ROWS, :].astype(jnp.int32).astype(F32).reshape(ROWS // GROUP, GROUP, TL)
+    return (x * scale[:, None, :]).reshape(SP, 64, TL)
+
+
+class PackedSpread(Spread):
+    def __init__(self, raw, *rest):
+        super().__init__(*rest)
+        self.raw = raw
+
+    def send1(self, p):
+        @pl.loop(1, 5)
+        def _(k):
+            q = (self.pos2 + k) % 4
+            pack(self.st.at[p, q], self.raw[p, q])
+            self.c1(p, q).start()
+
+    def add1(self):
+        @pl.loop(1, 5)
+        def _(k):
+            q = (self.pos2 + k) % 4
+            total = self.raw[self.pos1, q]
+            for o in (1, 2, 3):
+                self.c1((self.pos1 + o) % 4, q).wait_recv()
+            for o in (1, 2, 3):
+                total = total + unpack(self.r1.at[o - 1, q])
+            self.raw[self.pos1, q] = total
+
+            @pl.when(k < 4)
+            def _():
+                pack(self.st.at[self.pos1, q], total)
+                self.c2(q).start()
+
+    def add2(self):
+        total = self.raw[self.pos1, self.pos2]
+        for o in (1, 2, 3):
+            self.c2((self.pos2 + o) % 4).wait_recv()
+        for o in (1, 2, 3):
+            total = total + unpack(self.r2.at[o - 1])
+        pack(self.all.at[self.c, self.pos1, self.pos2], total)
+        for o in (2, 1, 3):
+            self.c3(o, self.pos2, self.dev2((self.pos2 - o + 4) % 4)).start()
+
+
 def rcopy(src, dst, ss, rs, device):
     return pltpu.make_async_remote_copy(
         src_ref=src, dst_ref=dst, send_sem=ss, recv_sem=rs, device_id=device, device_id_type=MESH
@@ -228,7 +289,7 @@
 
 
 def main_kernel(owner_ref, g_ref, acc_ref, new_ref, gs_ref, lroot_ref, rroot_ref, *scratch):
-    (praw, accn, sts, sr1, sr2, sall, stg, gr1, gr2, pacc, am, rsend), scratch = scratch[:12], scratch[12:]
+    (praw, accn, raws, sts, sr1, sr2, sall, stg, gr1, gr2, pacc, am, rsend), scratch = scratch[:13], scratch[13:]
     bufs, scratch = scratch[:12], scratch[12:]
     ssem, gsem, (s_raw, s_acc, s_old, s_root, s_new) = scratch[:10], scratch[10:20], scratch[20:]
     y, z, c = coords()
@@ -243,7 +304,7 @@
 
     mate = at(y, z, 1 - c)
     place = (c, pos1, pos2, dev1, dev2, mate)
-    stat = Spread(sts, sr1, sr2, sall, ssem, place)
+    stat = PackedSpread(raws, sts, sr1, sr2, sall, ssem, place)
     gsum = Spread(stg, gr1, gr2, gs_ref, gsem, place)
 
     olds = [pltpu.make_async_copy(acc_ref.at[j], accn.at[j], s_old.at[j]) for j in range(SLOTS)]
@@ -267,7 +328,7 @@
         t = TILES.index((a, b))
         for half in range(2):
             h = 2 * t + half
-            sts[p, h // SP, h % SP] = block[half * 64:(half + 1) * 64]
+            raws[p, h // SP, h % SP] = block[half * 64:(half + 1) * 64]
 
     def quadrants(p, quad):
         x = quad(0, 0)
@@ -344,14 +405,18 @@
     def blend(dst, src, blk, alive, lr):
         keep = jnp.where(alive == 1, F32(decay_rate), F32(1.0))
         take = jnp.where(alive == 1, F32((1.0 - decay_rate) / 16384.0), F32(0.0))
-        for t, (a, b) in enumerate(TILES):
-            for half in range(2):
-                h = 2 * t + half
-                fresh = take * sall[blk // 2, 2 * (blk % 2) + lr, h // SP, h % SP]
+        for q in range(4):
+            chunk = take * unpack(sall.at[blk // 2, 2 * (blk % 2) + lr, q])
+            for n in range(SP):
+                h = q * SP + n
+                a, b = TILES[h // 2]
+                half = h % 2
+                fresh = chunk[n]
                 ra, rb = pl.ds(a * TL + half * 64, 64), pl.ds(b * TL, TL)
                 dst[ra, rb] = keep * src[ra, rb] + fresh
                 if a != b:
-                    dst[rb, ra] = keep * src[rb, ra] + fresh.T
+                    ca = pl.ds(a * TL + half * 64, 64)
+                    dst[rb, ca] = keep * src[rb, ca] + fresh.T
 
     def root(j):
         return rcopy(rsend.at[j], rroot_ref.at[j], s_root.at[0, j], s_root.at[1, j], mate)
@@ -427,9 +492,10 @@
             square((2,), BF16),
             square((SLOTS, 2), F32),
             pltpu.VMEM((4, 4, SP, 64, TL), F32),
-            pltpu.VMEM((3, 4, SP, 64, TL), F32),
-            pltpu.VMEM((3, SP, 64, TL), F32),
-            pltpu.VMEM((2, 4, 4, SP, 64, TL), F32),
+            pltpu.VMEM((4, 4, PACKED, TL), jnp.int16),
+            pltpu.VMEM((3, 4, PACKED, TL), jnp.int16),
+            pltpu.VMEM((3, PACKED, TL), jnp.int16),
+            pltpu.VMEM((2, 4, 4, PACKED, TL), jnp.int16),
             pltpu.VMEM((4, 4, GP, 64, TL), F32),
             pltpu.VMEM((3, 4, GP, 64, TL), F32),
             pltpu.VMEM((3, GP, 64, TL), F32),

time: 143 us -> 128 us (0.90)
  Pallas kernels: 138 us -> 123 us
    pallas_call x1, Pallas kernels: 93.2 us -> 77.3 us  [call_main(): pl.pallas_call(main_kernel, name='main', out_shape=(jax.ShapeDtypeStruct(...]
where the time goes in v5:
time: 128 us
  Pallas kernels  123 us (96%)
  local copies, waits for them, and re-layouts  3.86 us (3%)
    pallas_call x1, Pallas kernels, call_main(): pl.pallas_call(main_kernel, name='main', out_shape=(jax.ShapeDtypeStruct(...  77.3 us
    pallas_call x1, Pallas kernels, call_tail(): pl.pallas_call(functools.partial(tail_kernel, n_mp), name='tail', out_sha...  41.8 us
    pallas_call x1, Pallas kernels, call_product(): pl.pallas_call(product_kernel, name='product', out_shape=(jax.ShapeDtypeS...  3.89 us
    unnamed x9, local copies, waits for them, and re-layouts  3.86 us

profile of v5, /device:TPU:1, one launch (start us, length us, event | category | flops | bytes accessed | tf_op | source)
XLA Modules:
  0.0 127.5 jit_solution(6716858737695484887)
XLA Ops:
  0.6 0.0 copy-start
  0.6 0.0 copy-start.1
  0.7 1.7 %copy-done.1 = bf16[1,4,512,512]{3,2,1,0:T(8,128)(2,1)S(1)} copy-done((bf16[1,4,512,512]{3,2,1,0:T(8,128)(2,1)S(1)}, bf16[1,4,512,512]{3,2,1,0:T(8,128)(2,1)}, u32[]{:S(2)}) %copy-start.1) | copy-done | bytes 2097176
  2.4 0.0 copy-start.2
  2.4 0.8 copy-done.2
  3.2 0.0 copy-start.3
  3.2 77.3 %main.1 = (f32[2,2,512,512]{3,2,1,0:T(8,128)S(1)}, f32[2,4,4,4,64,128]{5,4,3,2,1,0:T(8,128)S(1)}, f32[2,512,512]{2,1,0:T(8,128)S(1)}, f32[2,512,512]{2,1,0:T(8,128)S(1)}) custom-call(s32[1,4]{1,0:T(1,128)S(1)} %copy-done.2, bf16[4,512,512]{2,1,0:T(8,128)(2,1)S(1)} %bitcast.7, f32[2,2,512,512]{3,2,1,0:T(8,128)} %bitcast.9), custom_call_target="tpu_custom_call" | custom-call | tf_op jit(solution)/shard_map/main/pallas_call | solution.py:480
  80.5 0.0 copy-done
  80.5 0.0 copy-done.3
  80.5 3.9 %product.1 = (f32[2,2,512,512]{3,2,1,0:T(8,128)}, f32[2,2,512,512]{3,2,1,0:T(8,128)}, f32[8,128]{1,0:T(8,128)S(1)}, f32[2,512,512]{2,1,0:T(8,128)S(1)}) custom-call(s32[1,4]{1,0:T(1,128)S(1)} %copy-done.2, s32[1,2]{1,0:T(1,128)S(1)} %bitcast.8, f32[2,2,512,512]{3,2,1,0:T(8,128)S(1)} %get-tuple-element.11.new_ref, ...), custom_call_target="tpu_custom_call" | custom-call | tf_op jit(solution)/shard_map/product/pallas_call | solution.py:582
  84.4 41.8 %tail.1 = bf16[4,512,512]{2,1,0:T(8,128)(2,1)S(1)} custom-call(s32[1,4]{1,0:T(1,128)S(1)} %copy-done.2, f32[2,512,512]{2,1,0:T(8,128)S(1)} %get-tuple-element.17.p_ref, f32[8,128]{1,0:T(8,128)S(1)} %get-tuple-element.18.sq_ref), custom_call_target="tpu_custom_call" | custom-call | tf_op jit(solution)/shard_map/tail/pallas_call | solution.py:789
  126.2 1.3 %copy.9 = bf16[4,512,512]{2,1,0:T(8,128)(2,1)} copy(bf16[4,512,512]{2,1,0:T(8,128)(2,1)S(1)} %tail.1) | data formatting | bytes 4194304
Async XLA Ops:
  0.6 79.9 %copy-start = (f32[1,1,2,2,512,512]{5,4,3,2,1,0:T(8,128)S(1)}, f32[1,1,2,2,512,512]{5,4,3,2,1,0:T(8,128)}, u32[]{:S(2)}) copy-start(f32[1,1,2,2,512,512]{5,4,3,2,1,0:T(8,128)} %param.9) | copy-start | bytes 12582916
  0.6 1.7 %copy-start.1 = (bf16[1,4,512,512]{3,2,1,0:T(8,128)(2,1)S(1)}, bf16[1,4,512,512]{3,2,1,0:T(8,128)(2,1)}, u32[]{:S(2)}) copy-start(bf16[1,4,512,512]{3,2,1,0:T(8,128)(2,1)} %param.5) | copy-start | bytes 6291460
  2.4 0.8 copy-start.2
  3.2 77.3 %copy-start.3 = (s32[1,1,2]{2,1,0:T(1,128)S(1)}, s32[1,1,2]{2,1,0:T(1,128)}, u32[]{:S(2)}) copy-start(s32[1,1,2]{2,1,0:T(1,128)} %param.7) | copy-start | bytes 28

commit v6 on v5

--- a/solution.py
+++ b/solution.py
@@ -72,7 +72,7 @@
     return block, alive
 
 
-def inverse_root(a_ref, store, bufs):
+def inverse_root(a_ref, store, bufs, hook):
     mf, m2f, nf, zf, mh, ml, ah, al, bh, bl, ch, cl = bufs
     a = a_ref[...]
     square = jnp.sum(a * a, axis=0, keepdims=True)
@@ -111,8 +111,9 @@
         put(None, bh, None, q, r, k)
         put(None, ch, None, W4 * m + W5 * m2 + W6 * q, r, k)
 
-    multiply(ah, al, mh, ml, third)
+    multiply(ah, None, mh, None, third)
     multiply(ch, None, bh, None, lambda q, r, k: put(nf, ah, al, nf[r, k] + q, r, k))
+    hook()
     multiply(ah, al, mh, ml, lambda q, r, k: put(zf, ch, cl, W0 * mf[r, k] + q, r, k))
     multiply(ah, al, ah, al, lambda q, r, k: put(m2f, bh, bl, (2 * W0) * nf[r, k] + q, r, k))
     multiply(bh, bl, bh, bl, lambda q, r, k: put(None, ah, al, (2 * W0 * W0) * m2f[r, k] + q, r, k))
@@ -186,17 +187,26 @@
             q = (self.pos2 + k) % 4
             if k:
                 self.c3(k, q, self.dev2(q)).wait_recv()
-            for o in (2, 1, 3):
+            for o in (1, 3):
                 self.c4(o, self.pos1, q, self.dev1((self.pos1 - o + 4) % 4)).start()
             self.cd(self.c, self.pos1, q).start()
 
-    def gather1(self):
-        for o in (1, 3, 2):
-            p = (self.pos1 + o) % 4
-            for k in (0, 1, 3, 2):
-                q = (self.pos2 + k) % 4
+    def relay(self):
+        for k in (0, 1, 3, 2):
+            q = (self.pos2 + k) % 4
+            for o in (1, 3):
+                p = (self.pos1 + o) % 4
                 self.c4(o, p, q, self.dev1(p)).wait_recv()
+                if (o == 1) == (k < 2):
+                    self.c4(2, p, q, self.dev1((self.pos1 - o + 4) % 4)).start()
                 self.cd(self.c, p, q).start()
+
+    def finish(self):
+        p = (self.pos1 + 2) % 4
+        for k in (0, 1, 3, 2):
+            q = (self.pos2 + k) % 4
+            self.c4(2, p, q, self.dev1(p)).wait_recv()
+            self.cd(self.c, p, q).start()
 
     def from_mate(self):
         for p in range(4):
@@ -289,7 +299,7 @@
 
 
 def main_kernel(owner_ref, g_ref, acc_ref, new_ref, gs_ref, lroot_ref, rroot_ref, *scratch):
-    (praw, accn, raws, sts, sr1, sr2, sall, stg, gr1, gr2, pacc, am, rsend), scratch = scratch[:13], scratch[13:]
+    (praw, accs_v, raws, sts, sr1, sr2, sall, stg, gr1, gr2, rsend), scratch = scratch[:11], scratch[11:]
     bufs, scratch = scratch[:12], scratch[12:]
     ssem, gsem, (s_raw, s_acc, s_old, s_root, s_new) = scratch[:10], scratch[10:20], scratch[20:]
     y, z, c = coords()
@@ -307,7 +317,7 @@
     stat = PackedSpread(raws, sts, sr1, sr2, sall, ssem, place)
     gsum = Spread(stg, gr1, gr2, gs_ref, gsem, place)
 
-    olds = [pltpu.make_async_copy(acc_ref.at[j], accn.at[j], s_old.at[j]) for j in range(SLOTS)]
+    olds = [pltpu.make_async_copy(acc_ref.at[j, 0], accs_v.at[SLOTS + j], s_old.at[j]) for j in range(SLOTS)]
     for a in olds:
         a.start()
     barrier = pltpu.get_barrier_semaphore()
@@ -319,7 +329,7 @@
 
     raw = rcopy(g_ref.at[pl.ds(2 * (1 - c), 2)], praw, s_raw.at[0], s_raw.at[1], mate)
     raw.start()
-    accs = [rcopy(acc_ref.at[j, 1], pacc.at[j], s_acc.at[0, j], s_acc.at[1, j], mate) for j in range(SLOTS)]
+    accs = [rcopy(acc_ref.at[j, 1], accs_v.at[j], s_acc.at[0, j], s_acc.at[1, j], mate) for j in range(SLOTS)]
     raw.wait()
     for a in accs:
         a.start()
@@ -391,8 +401,8 @@
     stat.add2()
     stat.gather2()
     gsum.add1()
-    stat.gather1()
-    gsum.add2()
+    stat.relay()
+    stat.finish()
     for a in accs:
         a.wait()
     for a in olds:
@@ -402,7 +412,7 @@
     d = lax.axis_index("dp")
     other = d + 1 - 2 * c
 
-    def blend(dst, src, blk, alive, lr):
+    def blend(dst, blk, alive, lr):
         keep = jnp.where(alive == 1, F32(decay_rate), F32(1.0))
         take = jnp.where(alive == 1, F32((1.0 - decay_rate) / 16384.0), F32(0.0))
         for q in range(4):
@@ -413,33 +423,35 @@
                 half = h % 2
                 fresh = chunk[n]
                 ra, rb = pl.ds(a * TL + half * 64, 64), pl.ds(b * TL, TL)
-                dst[ra, rb] = keep * src[ra, rb] + fresh
+                dst[ra, rb] = keep * dst[ra, rb] + fresh
                 if a != b:
                     ca = pl.ds(a * TL + half * 64, 64)
-                    dst[rb, ca] = keep * src[rb, ca] + fresh.T
+                    dst[rb, ca] = keep * dst[rb, ca] + fresh.T
 
     def root(j):
         return rcopy(rsend.at[j], rroot_ref.at[j], s_root.at[0, j], s_root.at[1, j], mate)
 
-    def new(j):
-        return pltpu.make_async_copy(accn.at[j], new_ref.at[j], s_new.at[j])
+    def left(j):
+        return pltpu.make_async_copy(accs_v.at[SLOTS + j], new_ref.at[j, 0], s_new.at[0, j])
+
+    def right(j):
+        return rcopy(accs_v.at[j], new_ref.at[j, 1], s_new.at[1, j], s_new.at[2, j], mate)
 
     @pl.loop(0, 4)
     def _(t):
         j = t % 2
 
+        own = t // 2
+        blk, alive = find_slot(owner_ref, (other + own * (d - other)) * SLOTS + j)
+        blend(accs_v.at[t], blk, alive, 1 - own)
+
         @pl.when(t < 2)
         def _():
-            blk, _ = find_slot(owner_ref, other * SLOTS + j)
-            blend(am, pacc.at[j], blk, jnp.int32(1), 1)
+            right(j).start()
 
         @pl.when(t >= 2)
         def _():
-            blk, alive = find_slot(owner_ref, d * SLOTS + j)
-            blend(accn.at[j, 0], accn.at[j, 0], blk, alive, 0)
-            blend(accn.at[j, 1], accn.at[j, 1], blk, alive, 1)
-            am[...] = accn[j, 0]
-            new(j).start()
+            left(j).start()
 
         def store(rows, cols, x):
             @pl.when(t < 2)
@@ -450,23 +462,33 @@
             def _():
                 lroot_ref[j, rows, cols] = x
 
-        inverse_root(am, store, bufs)
+        def hook():
+            @pl.when(t == 0)
+            def _():
+                gsum.add2()
+
+            @pl.when(t == 2)
+            def _():
+                gsum.relay()
+
+            @pl.when(t == 3)
+            def _():
+                gsum.finish()
+
+        inverse_root(accs_v.at[t], store, bufs, hook)
+
+        @pl.when(t == 0)
+        def _():
+            gsum.gather2()
 
         @pl.when(t < 2)
         def _():
             root(j).start()
-
-        @pl.when(t == 0)
-        def _():
-            gsum.gather2()
-
-        @pl.when(t == 2)
-        def _():
-            gsum.gather1()
 
     for j in range(SLOTS):
         root(j).wait()
-        new(j).wait()
+        left(j).wait()
+        right(j).wait()
     gsum.from_mate()
     stat.sent()
     gsum.sent()
@@ -490,7 +512,7 @@
         out_specs=(hbm, vmem, vmem, vmem),
         scratch_shapes=[
             square((2,), BF16),
-            square((SLOTS, 2), F32),
+            square((2 * SLOTS,), F32),
             pltpu.VMEM((4, 4, SP, 64, TL), F32),
             pltpu.VMEM((4, 4, PACKED, TL), jnp.int16),
             pltpu.VMEM((3, 4, PACKED, TL), jnp.int16),
@@ -500,12 +522,10 @@
             pltpu.VMEM((3, 4, GP, 64, TL), F32),
             pltpu.VMEM((3, GP, 64, TL), F32),
             square((SLOTS,), F32),
-            square((), F32),
-            square((SLOTS,), F32),
         ]
         + [square((), F32)] * 4 + [square((), BF16)] * 8
         + Spread.sems() + Spread.sems()
-        + [dma((2,)), dma((2, SLOTS)), dma((SLOTS,)), dma((2, SLOTS)), dma((SLOTS,))],
+        + [dma((2,)), dma((2, SLOTS)), dma((SLOTS,)), dma((2, SLOTS)), dma((3, SLOTS))],
         compiler_params=pltpu.CompilerParams(
             collective_id=1, has_side_effects=True, vmem_limit_bytes=38 << 20
         ),
@@ -688,32 +708,32 @@
             n = n + (j - SLOTS) * (place == mate_base + j).astype(jnp.int32)
         index.append(n)
 
-    def c1(p, o):
-        return rcopy(sb.at[p], r1.at[o - 1], s1.at[o - 1], q1.at[o - 1], dev1(p))
+    def c1(p, o, q):
+        return rcopy(sb.at[p, q], r1.at[o - 1, q], s1.at[o - 1, q], q1.at[o - 1, q], dev1(p))
 
     @pl.loop(0, 4)
     def _(i):
         p = (pos1 + jnp.where(i == 0, 2, jnp.where(i == 1, 1, jnp.where(i == 2, 3, 0)))) % 4
         o = (pos1 - p + 4) % 4
-        for k in range(KB):
-            for q in range(4):
+        for n in range(1, 5):
+            q = (pos2 + n) % 4
+            for k in range(KB):
                 block = pbuf[index[k], pl.ds(p * 64 + q * 16, 16), :]
                 sb[p, q, k] = (ratio * block).astype(BF16)
 
-        @pl.when(i < 3)
-        def _():
-            c1(p, o).start()
+            @pl.when(i < 3)
+            def _():
+                c1(p, o, q).start()
 
     def c2(q):
         o = (pos2 - q + 4) % 4
         return rcopy(sb.at[pos1, q], r2.at[o - 1], s2.at[o - 1], q2.at[o - 1], dev2(q))
 
-    for o in (1, 2, 3):
-        c1(pos1, o).wait_recv()
-
     @pl.loop(1, 5)
     def _(k):
         q = (pos2 + k) % 4
+        for o in (1, 2, 3):
+            c1(pos1, o, q).wait_recv()
         sb[pos1, q] = (sb[pos1, q] + r1[0, q]) + (r1[1, q] + r1[2, q])
 
         @pl.when(k < 4)
@@ -751,16 +771,28 @@
         q = (pos2 + k) % 4
         if k:
             rcopy(f3.at[pos2], f3.at[q], s3.at[k - 1], q3.at[k - 1], dev2(q)).wait_recv()
-        for o in (2, 1, 3):
+        for o in (1, 3):
             c4(o, q).start()
         cd_own(q).start()
         keep(q).start()
-    for o in (1, 3, 2):
-        for k in (0, 1, 3, 2):
-            q = (pos2 + k) % 4
+
+    def onward(o, q):
+        ref = out(c, (pos1 + o) % 4, q)
+        return rcopy(ref, ref, s4.at[1, q], q4.at[1, q], dev1((pos1 - o + 4) % 4))
+
+    for k in (0, 1, 3, 2):
+        q = (pos2 + k) % 4
+        for o in (1, 3):
             p = (pos1 + o) % 4
             rcopy(f3.at[q], out(c, p, q), s4.at[o - 1, q], q4.at[o - 1, q], dev1(p)).wait_recv()
+            if (o == 1) == (k < 2):
+                onward(o, q).start()
             cd(o, q).start()
+    for k in (0, 1, 3, 2):
+        q = (pos2 + k) % 4
+        p = (pos1 + 2) % 4
+        rcopy(out(c, p, q), out(c, p, q), s4.at[1, q], q4.at[1, q], dev1(p)).wait_recv()
+        cd(2, q).start()
 
     for o in range(1, 16):
         ca(o).wait_send()
@@ -770,15 +802,18 @@
         halves(j).wait_send()
     for k in range(1, 4):
         p = (pos1 + k) % 4
-        c1(p, (pos1 - p + 4) % 4).wait_send()
+        for q in range(4):
+            c1(p, (pos1 - p + 4) % 4, q).wait_send()
         c2((pos2 + k) % 4).wait_send()
         c3(k).wait_send()
     for q in range(4):
         keep(q).wait()
+        for o in (1, 3):
+            c4(o, q).wait_send()
         for o in (1, 2, 3):
-            c4(o, q).wait_send()
             cd(o, q).wait_send()
         cd_own(q).wait_send()
+        onward(1, q).wait_send()
         for o in range(4):
             p = (pos2 + o) % 4
             rcopy(f3.at[q], out(1 - c, p, q), sd.at[o, q], qd.at[o, q], mate).wait_recv()
@@ -802,7 +837,7 @@
             pltpu.VMEM((4, KB, 16, BS), BF16),
             dma((15,)), dma((15,)), dma((2 * n_mp - 1,)), dma((2 * n_mp - 1,)),
             dma((SLOTS,)), dma((SLOTS,)), dma((SLOTS,)),
-            dma((3,)), dma((3,)), dma((3,)), dma((3,)), dma((3,)), dma((3,)),
+            dma((3, 4)), dma((3, 4)), dma((3,)), dma((3,)), dma((3,)), dma((3,)),
             dma((3, 4)), dma((3, 4)), dma((4, 4)), dma((4, 4)), dma((4,)),
         ],
         compiler_params=pltpu.CompilerParams(

time: 128 us -> 127 us (level)
  Pallas kernels: 123 us -> 121 us
    pallas_call x1, Pallas kernels: 77.3 us -> 75.2 us  [call_main(): pl.pallas_call(main_kernel, name='main', out_shape=(jax.ShapeDtypeStruct(...]
where the time goes in v6:
time: 127 us; the launch traced here: 126 us
  Pallas kernels  121 us (95%)
  local copies, waits for them, and re-layouts  3.86 us (3%)
    pallas_call x1, Pallas kernels, call_main(): pl.pallas_call(main_kernel, name='main', out_shape=(jax.ShapeDtypeStruct(...  75.2 us
    pallas_call x1, Pallas kernels, call_tail(): pl.pallas_call(functools.partial(tail_kernel, n_mp), name='tail', out_sha...  42.3 us
    pallas_call x1, Pallas kernels, call_product(): pl.pallas_call(product_kernel, name='product', out_shape=(jax.ShapeDtypeS...  3.89 us
    unnamed x9, local copies, waits for them, and re-layouts  3.86 us

profile of v6, /device:TPU:1, one launch (start us, length us, event | category | flops | bytes accessed | tf_op | source)
XLA Modules:
  0.0 126.0 jit_solution(7965077662804915763)
XLA Ops:
  0.6 0.0 copy-start
  0.6 0.0 copy-start.1
  0.7 1.7 %copy-done.1 = bf16[1,4,512,512]{3,2,1,0:T(8,128)(2,1)S(1)} copy-done((bf16[1,4,512,512]{3,2,1,0:T(8,128)(2,1)S(1)}, bf16[1,4,512,512]{3,2,1,0:T(8,128)(2,1)}, u32[]{:S(2)}) %copy-start.1) | copy-done | bytes 2097176
  2.4 0.0 copy-start.2
  2.4 0.8 copy-done.2
  3.2 0.0 copy-start.3
  3.2 75.2 %main.1 = (f32[2,2,512,512]{3,2,1,0:T(8,128)S(1)}, f32[2,4,4,4,64,128]{5,4,3,2,1,0:T(8,128)S(1)}, f32[2,512,512]{2,1,0:T(8,128)S(1)}, f32[2,512,512]{2,1,0:T(8,128)S(1)}) custom-call(s32[1,4]{1,0:T(1,128)S(1)} %copy-done.2, bf16[4,512,512]{2,1,0:T(8,128)(2,1)S(1)} %bitcast.7, f32[2,2,512,512]{3,2,1,0:T(8,128)} %bitcast.9), custom_call_target="tpu_custom_call" | custom-call | tf_op jit(solution)/shard_map/main/pallas_call | solution.py:502
  78.4 0.0 copy-done
  78.4 0.0 copy-done.3
  78.4 3.9 %product.1 = (f32[2,2,512,512]{3,2,1,0:T(8,128)}, f32[2,2,512,512]{3,2,1,0:T(8,128)}, f32[8,128]{1,0:T(8,128)S(1)}, f32[2,512,512]{2,1,0:T(8,128)S(1)}) custom-call(s32[1,4]{1,0:T(1,128)S(1)} %copy-done.2, s32[1,2]{1,0:T(1,128)S(1)} %bitcast.8, f32[2,2,512,512]{3,2,1,0:T(8,128)S(1)} %get-tuple-element.11.new_ref, ...), custom_call_target="tpu_custom_call" | custom-call | tf_op jit(solution)/shard_map/product/pallas_call | solution.py:602
  82.3 42.3 %tail.1 = bf16[4,512,512]{2,1,0:T(8,128)(2,1)S(1)} custom-call(s32[1,4]{1,0:T(1,128)S(1)} %copy-done.2, f32[2,512,512]{2,1,0:T(8,128)S(1)} %get-tuple-element.17.p_ref, f32[8,128]{1,0:T(8,128)S(1)} %get-tuple-element.18.sq_ref), custom_call_target="tpu_custom_call" | custom-call | tf_op jit(solution)/shard_map/tail/pallas_call | solution.py:824
  124.7 1.3 %copy.9 = bf16[4,512,512]{2,1,0:T(8,128)(2,1)} copy(bf16[4,512,512]{2,1,0:T(8,128)(2,1)S(1)} %tail.1) | data formatting | bytes 4194304
Async XLA Ops:
  0.6 77.8 %copy-start = (f32[1,1,2,2,512,512]{5,4,3,2,1,0:T(8,128)S(1)}, f32[1,1,2,2,512,512]{5,4,3,2,1,0:T(8,128)}, u32[]{:S(2)}) copy-start(f32[1,1,2,2,512,512]{5,4,3,2,1,0:T(8,128)} %param.9) | copy-start | bytes 12582916
  0.6 1.7 %copy-start.1 = (bf16[1,4,512,512]{3,2,1,0:T(8,128)(2,1)S(1)}, bf16[1,4,512,512]{3,2,1,0:T(8,128)(2,1)}, u32[]{:S(2)}) copy-start(bf16[1,4,512,512]{3,2,1,0:T(8,128)(2,1)} %param.5) | copy-start | bytes 6291460
  2.4 0.8 copy-start.2
  3.2 75.2 %copy-start.3 = (s32[1,1,2]{2,1,0:T(1,128)S(1)}, s32[1,1,2]{2,1,0:T(1,128)}, u32[]{:S(2)}) copy-start(s32[1,1,2]{2,1,0:T(1,128)} %param.7) | copy-start | bytes 28

commit v7 on v6

--- a/solution.py
+++ b/solution.py
@@ -329,18 +329,20 @@
 
     raw = rcopy(g_ref.at[pl.ds(2 * (1 - c), 2)], praw, s_raw.at[0], s_raw.at[1], mate)
     raw.start()
-    accs = [rcopy(acc_ref.at[j, 1], accs_v.at[j], s_acc.at[0, j], s_acc.at[1, j], mate) for j in range(SLOTS)]
-    raw.wait()
-    for a in accs:
-        a.start()
-
-    def put(p, a, b, block):
+
+    def first(p, a, b, block):
         t = TILES.index((a, b))
         for half in range(2):
             h = 2 * t + half
             raws[p, h // SP, h % SP] = block[half * 64:(half + 1) * 64]
 
-    def quadrants(p, quad):
+    def second(p, a, b, block):
+        t = TILES.index((a, b))
+        for half in range(2):
+            h = 2 * t + half
+            raws[p, h // SP, h % SP] += block[half * 64:(half + 1) * 64]
+
+    def quadrants(put, p, quad):
         x = quad(0, 0)
         put(p, 0, 0, x[:128, :128])
         put(p, 0, 1, x[:128, 128:])
@@ -355,30 +357,34 @@
         put(p, 2, 3, x[:128, 128:])
         put(p, 3, 3, x[128:, 128:])
 
+    def statistic(put, p, ref, blk):
+        @pl.when(p % 2 == 0)
+        def _():
+            quadrants(
+                put, p,
+                lambda a, b: dot_nt(ref[blk, a * 256:(a + 1) * 256, :], ref[blk, b * 256:(b + 1) * 256, :]),
+            )
+
+        @pl.when(p % 2 == 1)
+        def _():
+            quadrants(
+                put, p,
+                lambda a, b: dot_tn(ref[blk, :, a * 256:(a + 1) * 256], ref[blk, :, b * 256:(b + 1) * 256]),
+            )
+
+    @pl.loop(0, 4)
+    def _(p):
+        statistic(first, p, g_ref, 2 * c + p // 2)
+
+    accs = [rcopy(acc_ref.at[j, 1], accs_v.at[j], s_acc.at[0, j], s_acc.at[1, j], mate) for j in range(SLOTS)]
+    raw.wait()
+    for a in accs:
+        a.start()
+
     @pl.loop(0, 4)
     def _(i):
         p = (pos1 + jnp.where(i == 0, 2, jnp.where(i == 1, 1, jnp.where(i == 2, 3, 0)))) % 4
-        blk = p // 2
-
-        @pl.when(p % 2 == 0)
-        def _():
-            quadrants(
-                p,
-                lambda a, b: dot_nt(
-                    g_ref[2 * c + blk, a * 256:(a + 1) * 256, :], g_ref[2 * c + blk, b * 256:(b + 1) * 256, :]
-                )
-                + dot_nt(praw[blk, a * 256:(a + 1) * 256, :], praw[blk, b * 256:(b + 1) * 256, :]),
-            )
-
-        @pl.when(p % 2 == 1)
-        def _():
-            quadrants(
-                p,
-                lambda a, b: dot_tn(
-                    g_ref[2 * c + blk, :, a * 256:(a + 1) * 256], g_ref[2 * c + blk, :, b * 256:(b + 1) * 256]
-                )
-                + dot_tn(praw[blk, :, a * 256:(a + 1) * 256], praw[blk, :, b * 256:(b + 1) * 256]),
-            )
+        statistic(second, p, praw, p // 2)
 
         @pl.when(i < 3)
         def _():

time: 127 us -> 127 us (level)
  no operation moved by 1% of the time
where the time goes in v7:
time: 127 us; the launch traced here: 126 us
  Pallas kernels  122 us (96%)
  local copies, waits for them, and re-layouts  3.86 us (3%)
    pallas_call x1, Pallas kernels, call_main(): pl.pallas_call(main_kernel, name='main', out_shape=(jax.ShapeDtypeStruct(...  75 us
    pallas_call x1, Pallas kernels, call_tail(): pl.pallas_call(functools.partial(tail_kernel, n_mp), name='tail', out_sha...  43 us
    pallas_call x1, Pallas kernels, call_product(): pl.pallas_call(product_kernel, name='product', out_shape=(jax.ShapeDtypeS...  3.89 us
    unnamed x9, local copies, waits for them, and re-layouts  3.86 us

profile of v7, /device:TPU:1, one launch (start us, length us, event | category | flops | bytes accessed | tf_op | source)
XLA Modules:
  0.0 126.5 jit_solution(17721615492787977049)
XLA Ops:
  0.6 0.0 copy-start
  0.6 0.0 copy-start.1
  0.7 1.7 %copy-done.1 = bf16[1,4,512,512]{3,2,1,0:T(8,128)(2,1)S(1)} copy-done((bf16[1,4,512,512]{3,2,1,0:T(8,128)(2,1)S(1)}, bf16[1,4,512,512]{3,2,1,0:T(8,128)(2,1)}, u32[]{:S(2)}) %copy-start.1) | copy-done | bytes 2097176
  2.4 0.0 copy-start.2
  2.4 0.8 copy-done.2
  3.2 0.0 copy-start.3
  3.2 75.0 %main.1 = (f32[2,2,512,512]{3,2,1,0:T(8,128)S(1)}, f32[2,4,4,4,64,128]{5,4,3,2,1,0:T(8,128)S(1)}, f32[2,512,512]{2,1,0:T(8,128)S(1)}, f32[2,512,512]{2,1,0:T(8,128)S(1)}) custom-call(s32[1,4]{1,0:T(1,128)S(1)} %copy-done.2, bf16[4,512,512]{2,1,0:T(8,128)(2,1)S(1)} %bitcast.7, f32[2,2,512,512]{3,2,1,0:T(8,128)} %bitcast.9), custom_call_target="tpu_custom_call" | custom-call | tf_op jit(solution)/shard_map/main/pallas_call | solution.py:508
  78.2 0.0 copy-done
  78.2 0.0 copy-done.3
  78.2 3.9 %product.1 = (f32[2,2,512,512]{3,2,1,0:T(8,128)}, f32[2,2,512,512]{3,2,1,0:T(8,128)}, f32[8,128]{1,0:T(8,128)S(1)}, f32[2,512,512]{2,1,0:T(8,128)S(1)}) custom-call(s32[1,4]{1,0:T(1,128)S(1)} %copy-done.2, s32[1,2]{1,0:T(1,128)S(1)} %bitcast.8, f32[2,2,512,512]{3,2,1,0:T(8,128)S(1)} %get-tuple-element.11.new_ref, ...), custom_call_target="tpu_custom_call" | custom-call | tf_op jit(solution)/shard_map/product/pallas_call | solution.py:608
  82.1 43.0 %tail.1 = bf16[4,512,512]{2,1,0:T(8,128)(2,1)S(1)} custom-call(s32[1,4]{1,0:T(1,128)S(1)} %copy-done.2, f32[2,512,512]{2,1,0:T(8,128)S(1)} %get-tuple-element.17.p_ref, f32[8,128]{1,0:T(8,128)S(1)} %get-tuple-element.18.sq_ref), custom_call_target="tpu_custom_call" | custom-call | tf_op jit(solution)/shard_map/tail/pallas_call | solution.py:830
  125.2 1.3 %copy.9 = bf16[4,512,512]{2,1,0:T(8,128)(2,1)} copy(bf16[4,512,512]{2,1,0:T(8,128)(2,1)S(1)} %tail.1) | data formatting | bytes 4194304
Async XLA Ops:
  0.6 77.6 %copy-start = (f32[1,1,2,2,512,512]{5,4,3,2,1,0:T(8,128)S(1)}, f32[1,1,2,2,512,512]{5,4,3,2,1,0:T(8,128)}, u32[]{:S(2)}) copy-start(f32[1,1,2,2,512,512]{5,4,3,2,1,0:T(8,128)} %param.9) | copy-start | bytes 12582916
  0.6 1.7 %copy-start.1 = (bf16[1,4,512,512]{3,2,1,0:T(8,128)(2,1)S(1)}, bf16[1,4,512,512]{3,2,1,0:T(8,128)(2,1)}, u32[]{:S(2)}) copy-start(bf16[1,4,512,512]{3,2,1,0:T(8,128)(2,1)} %param.5) | copy-start | bytes 6291460
  2.4 0.8 copy-start.2
  3.2 75.0 %copy-start.3 = (s32[1,1,2]{2,1,0:T(1,128)S(1)}, s32[1,1,2]{2,1,0:T(1,128)}, u32[]{:S(2)}) copy-start(s32[1,1,2]{2,1,0:T(1,128)} %param.7) | copy-start | bytes 28
